TPU v7x, 512 devices: a whole 4x8x8 slice. The times are simulated.
512 devices in a mesh: tile: 16 (over y, core), slab: 32 (over z, x).
Axes of the slice: x: 4, y: 8, z: 8, core: 2. Of those that a mesh axis runs over, the one named last changes fastest.
Arguments:
- field: float32 [512, 1024, 512], P('slab', 'tile'), may hold values from -6 to 6
- arc_ids: int32 [512, 1024, 512], P('slab', 'tile'), may hold values from 0 to 63
- arc_tf: int32 [64], replicated, may hold values from 0 to 15
- tf_table: bfloat16 [6, 16], replicated, may hold values from -2 to 12, as said below
Outputs:
- frame: float32 [4, 1024, 512], P(None, 'tile')
Inputs may be any that keep to these rules, and one draw needn't show every extreme that they name: `tf_table`: rows 0 to 2 are colours in 0 to 1, row 3 an extinction in 0.3 to 12, row 4 a centre value in -2 to 2, row 5 an inverse width in 0.4 to 1.5.
All inputs are finite; a program needn't handle non-finite values.
Results may differ from a plain program's by a relative error of at most 0.0003.
Values sent between devices are 32-bit elements; how exact they have to be, the bound alone decides.
No kernel may reach another device: no remote copies, remote signals or barrier semaphores. Data moves between devices by JAX's collectives and lax.ppermute only.
A program may use at most 128 MiB of HBM per device.

v0:
```python
import math

import jax
import jax.numpy as jnp
import numpy as np
from jax import lax
from jax.sharding import PartitionSpec as P


def with_halo(block, sides, width):
    for axis, dim in sides:
        count = lax.axis_size(axis)
        forward = [(i, i + 1) for i in range(count - 1)]
        backward = [(target, source) for source, target in forward]
        low = lax.ppermute(
            lax.slice_in_dim(block, block.shape[dim] - width, None, axis=dim), axis, forward
        )
        high = lax.ppermute(lax.slice_in_dim(block, 0, width, axis=dim), axis, backward)
        block = jnp.concatenate([low, block, high], axis=dim)
    return block


def swapped(value, axis, distance):
    mask = 2**distance
    pairs = [(source, source ^ mask) for source in range(lax.axis_size(axis))]
    return lax.ppermute(value, axis, pairs)


def optics(center, slope_across, slope_down, slope_depth, looked, step_len):
    lambert = 0.48 * slope_across + 0.6 * slope_down + 0.64 * slope_depth
    shading = 0.35 + 0.65 * jnp.abs(lambert) / jnp.sqrt(
        1.0 + slope_across * slope_across + slope_down * slope_down + slope_depth * slope_depth
    )
    extinction = looked[3] * jnp.exp(-jnp.square(looked[5] * (center - looked[4])))
    passing = jnp.exp(-extinction * step_len)
    weight = (1.0 - passing) * shading
    return (passing, weight[None] * looked[:3])


def composite(front_part, back_part):
    colour = front_part[..., :3, :] + front_part[..., 3:, :] * back_part[..., :3, :]
    transmit = front_part[..., 3:, :] * back_part[..., 3:, :]
    return jnp.concatenate([colour, transmit], axis=-2)


def local(field, arc_ids, arc_tf, tf_table):
    depth_cells, tile_rows, columns = field.shape
    slab_count = lax.axis_size("slab")
    step_len = 2.0 / (depth_cells * slab_count)
    tf_count = tf_table.shape[1]
    arc_count = arc_tf.shape[0]
    tf_select = (arc_tf[None, :] == jnp.arange(tf_count, dtype=jnp.int32)[:, None]).astype(
        jnp.bfloat16
    )
    arc_params = jnp.dot(tf_table, tf_select, preferred_element_type=jnp.float32).astype(
        jnp.bfloat16
    )
    arc_range = jnp.arange(arc_count, dtype=jnp.int32)[:, None]
    padded = with_halo(field, (("tile", 1), ("slab", 0)), 1)
    group = math.gcd(depth_cells, max(1, 32768 // (tile_rows * columns)))
    block_count = depth_cells // group

    def advance(totals, block_index):
        colour, transmit = totals
        first_layer = block_index * group
        block = lax.dynamic_slice_in_dim(padded, first_layer, group + 2, 0)
        arc_block = lax.dynamic_slice_in_dim(arc_ids, first_layer, group, 0)
        center = block[1:-1, 1:-1]
        slope_depth = (block[2:, 1:-1] - block[:-2, 1:-1]) * 0.5
        slope_down = (block[1:-1, 2:] - block[1:-1, :-2]) * 0.5
        widened = jnp.pad(center, ((0, 0), (0, 0), (1, 1)))
        slope_across = (widened[:, :, 2:] - widened[:, :, :-2]) * 0.5
        one_hot = (arc_block.reshape(-1)[None, :] == arc_range).astype(jnp.bfloat16)
        looked = jnp.dot(arc_params, one_hot, preferred_element_type=jnp.float32).reshape(
            (6,) + center.shape
        )
        passing, emitted = optics(center, slope_across, slope_down, slope_depth, looked, step_len)
        running = jnp.cumprod(passing, axis=0)
        before = jnp.concatenate([jnp.ones_like(running), running[:-1]], axis=0)
        colour = colour + transmit[None] * jnp.sum(before[None] * emitted, axis=1)
        transmit = transmit * running[-1]
        return ((colour, transmit), None)

    start_totals = (
        jnp.zeros((3, tile_rows, columns), jnp.float32),
        jnp.ones((tile_rows, columns), jnp.float32),
    )
    final_totals, ignored = lax.scan(
        advance, start_totals, jnp.arange(block_count, dtype=jnp.int32)
    )
    colour, transmit = final_totals
    partial_value = jnp.concatenate([colour, transmit[None]], axis=0).reshape(4, -1)
    sections = slab_count.bit_length() - 1
    my_index = lax.axis_index("slab")
    image_part = partial_value
    for section_num in range(sections):
        half_len = image_part.shape[1] // 2
        lower_half = image_part[:, :half_len]
        upper_half = image_part[:, half_len:]
        is_back = my_index // 2**section_num % 2 == 1
        outgoing = jnp.where(is_back, lower_half, upper_half)
        arrived = swapped(outgoing, "slab", section_num)
        kept_half = jnp.where(is_back, upper_half, lower_half)
        front_part = jnp.where(is_back, arrived, kept_half)
        back_part = jnp.where(is_back, kept_half, arrived)
        image_part = composite(front_part, back_part)
    ordering = np.array(
        [
            sum(
                ((position >> bit_pos & 1) << sections - 1 - bit_pos for bit_pos in range(sections))
            )
            for position in range(slab_count)
        ],
        dtype=np.int32,
    )
    collected = lax.all_gather(image_part, "slab", axis=1, tiled=True)
    pieces = collected.reshape(4, slab_count, -1)[:, ordering]
    finished = pieces.reshape(4, tile_rows, columns)
    return jnp.concatenate([finished[:3], 1.0 - finished[3:]], axis=0)


def solution(mesh):
    in_specs = (P("slab", "tile", None), P("slab", "tile", None), P(), P())
    out_specs = P(None, "tile", None)
    return jax.shard_map(local, mesh=mesh, in_specs=in_specs, out_specs=out_specs, check_vma=False)
```

profile of v0, /device:TPU:8, one launch (start us, length us, event | category | flops | bytes accessed | tf_op | source)
XLA Modules:
  0.0 280.7 jit_solution(14277269391190633485)
XLA Ops:
  1.2 1.9 collective-permute-start
  3.2 3.6 %collective-permute-start.1 = (f32[16,1,512]{2,1,0:T(1,128)S(1)}, f32[16,1,512]{2,1,0:T(1,128)S(1)}, u32[]{:S(2)}, u32[]{:S(2)}) collective-permute-start(f32[16,1,512]{2,1,0:T(1,128)S(1)} %get-tuple-element.170), channel_id=1, source_target_pairs={{32,0},{64,32},{96,64},{128,96},{160,128},{192,160},{224,192},{256... | collective-permute-start | bytes 98312 | tf_op jit(solution)/shard_map/ppermute | solution.py:18
  6.9 1.5 collective-permute-done.1
  9.4 3.4 %collective-permute-start.2 = (f32[1,66,512]{2,1,0:T(8,128)S(1)}, f32[1,66,512]{2,1,0:T(8,128)S(1)}, u32[]{:S(2)}, u32[]{:S(2)}) collective-permute-start(f32[1,66,512]{2,1,0:T(8,128)S(1)} %get-tuple-element.167), channel_id=1, source_target_pairs={{0,1},{1,2},{2,3},{3,4},{4,5},{5,6},{6,7},{7,8},{8,9},{9,10},{10,1... | collective-permute-start | bytes 405512 | tf_op jit(solution)/shard_map/ppermute | solution.py:15
  14.9 1.4 collective-permute-done.2
  16.3 4.7 %collective-permute-done.3 = f32[1,66,512]{2,1,0:T(8,128)S(1)} collective-permute-done((f32[1,66,512]{2,1,0:T(8,128)S(1)}, f32[1,66,512]{2,1,0:T(8,128)S(1)}, u32[]{:S(2)}, u32[]{:S(2)}) %collective-permute-start.3) | collective-permute-done | bytes 135200 | tf_op jit(solution)/shard_map/ppermute | solution.py:18
  21.1 2.0 pad_maximum_fusion
  23.1 154.8 %while.15 = (s32[]{:T(128)}, f32[3,64,512]{2,1,0:T(8,128)S(1)}, f32[64,512]{1,0:T(8,128)S(1)}, s32[16]{0:T(128)S(1)}, s32[16,64,512]{2,1,0:T(8,128)}, /*index=5*...) while((s32[]{:T(128)}, f32[3,64,512]{2,1,0:T(8,128)S(1)}, ...), condition=%wide.region_2.3_spmd.clone, body=%wide.region_0.2_spmd.clone.sunk | while | flops 28704772 | bytes 7472159 | solution.py:88
  28.4 1.3 convolution_bitcast_fusion.2
  30.9 1.4 multiply_bitcast_fusion.2
  38.0 1.3 convolution_bitcast_fusion.2
  40.6 1.4 multiply_bitcast_fusion.2
  50.2 1.4 multiply_bitcast_fusion.2
  57.4 1.3 convolution_bitcast_fusion.2
  59.9 1.4 multiply_bitcast_fusion.2
  67.1 1.3 convolution_bitcast_fusion.2
  69.6 1.4 multiply_bitcast_fusion.2
  76.8 1.3 convolution_bitcast_fusion.2
  79.3 1.4 multiply_bitcast_fusion.2
  86.4 1.3 convolution_bitcast_fusion.2
  88.9 1.4 multiply_bitcast_fusion.2
  98.6 1.4 multiply_bitcast_fusion.2
  105.8 1.3 convolution_bitcast_fusion.2
  108.3 1.4 multiply_bitcast_fusion.2
  115.5 1.3 convolution_bitcast_fusion.2
  118.0 1.4 multiply_bitcast_fusion.2
  125.1 1.3 convolution_bitcast_fusion.2
  127.7 1.4 multiply_bitcast_fusion.2
  134.8 1.3 convolution_bitcast_fusion.2
  137.3 1.4 multiply_bitcast_fusion.2
  144.5 1.3 convolution_bitcast_fusion.2
  147.0 1.4 multiply_bitcast_fusion.2
  154.2 1.3 convolution_bitcast_fusion.2
  156.7 1.4 multiply_bitcast_fusion.2
  163.8 1.3 convolution_bitcast_fusion.2
  166.4 1.4 multiply_bitcast_fusion.2
  176.0 1.4 multiply_bitcast_fusion.2
  178.5 3.4 %collective-permute-start.4 = (f32[4,16384]{1,0:T(4,128)S(1)}, f32[4,16384]{1,0:T(4,128)S(1)}, u32[]{:S(2)}, u32[]{:S(2)}) collective-permute-start(f32[4,16384]{1,0:T(4,128)S(1)} %get-tuple-element.165), channel_id=1, source_target_pairs={{0,1},{1,0},{2,3},{3,2},{4,5},{5,4},{6,7},{7,6},{8,9},{9,8},{10,11... | collective-permute-start | bytes 786440 | tf_op jit(solution)/shard_map/ppermute | solution.py:26
  182.0 6.8 %collective-permute-done.4 = f32[4,16384]{1,0:T(4,128)S(1)} collective-permute-done((f32[4,16384]{1,0:T(4,128)S(1)}, f32[4,16384]{1,0:T(4,128)S(1)}, u32[]{:S(2)}, u32[]{:S(2)}) %collective-permute-start.4) | collective-permute-done | bytes 262176 | tf_op jit(solution)/shard_map/ppermute | solution.py:26
  189.4 7.3 %collective-permute-start.5 = (f32[4,8192]{1,0:T(4,128)S(1)}, f32[4,8192]{1,0:T(4,128)S(1)}, u32[]{:S(2)}, u32[]{:S(2)}) collective-permute-start(f32[4,8192]{1,0:T(4,128)S(1)} %get-tuple-element.163), channel_id=1, source_target_pairs={{0,2},{1,3},{2,0},{3,1},{4,6},{5,7},{6,4},{7,5},{8,10},{9,11},{10,... | collective-permute-start | bytes 393224 | tf_op jit(solution)/shard_map/ppermute | solution.py:26
  196.7 3.3 %collective-permute-done.5 = f32[4,8192]{1,0:T(4,128)S(1)} collective-permute-done((f32[4,8192]{1,0:T(4,128)S(1)}, f32[4,8192]{1,0:T(4,128)S(1)}, u32[]{:S(2)}, u32[]{:S(2)}) %collective-permute-start.5) | collective-permute-done | bytes 131104 | tf_op jit(solution)/shard_map/ppermute | solution.py:26
  200.3 4.3 %collective-permute-start.6 = (f32[4,4096]{1,0:T(4,128)S(1)}, f32[4,4096]{1,0:T(4,128)S(1)}, u32[]{:S(2)}, u32[]{:S(2)}) collective-permute-start(f32[4,4096]{1,0:T(4,128)S(1)} %get-tuple-element.161), channel_id=1, source_target_pairs={{0,4},{1,5},{2,6},{3,7},{4,0},{5,1},{6,2},{7,3},{8,12},{9,13},{10,... | collective-permute-start | bytes 196616 | tf_op jit(solution)/shard_map/ppermute | solution.py:26
  204.7 2.2 collective-permute-done.6
  207.0 8.5 %collective-permute-start.7 = (f32[4,2048]{1,0:T(4,128)S(1)}, f32[4,2048]{1,0:T(4,128)S(1)}, u32[]{:S(2)}, u32[]{:S(2)}) collective-permute-start(f32[4,2048]{1,0:T(4,128)S(1)} %get-tuple-element.159), channel_id=1, source_target_pairs={{0,8},{1,9},{2,10},{3,11},{4,12},{5,13},{6,14},{7,15},{8,0},{9,1},... | collective-permute-start | bytes 98312 | tf_op jit(solution)/shard_map/ppermute | solution.py:26
  215.6 1.8 collective-permute-done.7
  217.5 6.4 %collective-permute-start.8 = (f32[4,1024]{1,0:T(4,128)S(1)}, f32[4,1024]{1,0:T(4,128)S(1)}, u32[]{:S(2)}, u32[]{:S(2)}) collective-permute-start(f32[4,1024]{1,0:T(4,128)S(1)} %get-tuple-element.157), channel_id=1, source_target_pairs={{0,16},{1,17},{2,18},{3,19},{4,20},{5,21},{6,22},{7,23},{8,24},{9,... | collective-permute-start | bytes 49160 | tf_op jit(solution)/shard_map/ppermute | solution.py:26
  224.0 3.1 %collective-permute-done.8 = f32[4,1024]{1,0:T(4,128)S(1)} collective-permute-done((f32[4,1024]{1,0:T(4,128)S(1)}, f32[4,1024]{1,0:T(4,128)S(1)}, u32[]{:S(2)}, u32[]{:S(2)}) %collective-permute-start.8) | collective-permute-done | bytes 16416 | tf_op jit(solution)/shard_map/ppermute | solution.py:26
  227.2 51.1 %all_gather.3 = f32[4,32768]{1,0:T(4,128)S(1)} all-gather(f32[4,1024]{1,0:T(4,128)S(1)} %pad_maximum_fusion.10), channel_id=1, replica_groups=mesh['tile'=16,'slab'=32] {'slab'}, dimensions={1}, use_global_device_ids=true | all-gather | bytes 540672 | tf_op jit(solution)/shard_map/all_gather | solution.py:116
  (239 shorter events, 77.3 us)
Async XLA Ops:
  0.0 14.1 %copy-start = (bf16[6,16]{1,0:T(8,128)(2,1)S(1)}, bf16[6,16]{1,0:T(8,128)(2,1)}, u32[]{:S(2)}) copy-start(bf16[6,16]{1,0:T(8,128)(2,1)} %param.11) | copy-start | bytes 580
  0.0 21.1 %copy-start.1 = (f32[16,64,512]{2,1,0:T(8,128)S(1)}, f32[16,64,512]{2,1,0:T(8,128)}, u32[]{:S(2)}) copy-start(f32[16,64,512]{2,1,0:T(8,128)} %param.8) | copy-start | bytes 6291460
  1.2 5.6 %collective-permute-start = (f32[16,1,512]{2,1,0:T(1,128)S(1)}, f32[16,1,512]{2,1,0:T(1,128)S(1)}, u32[]{:S(2)}, u32[]{:S(2)}) collective-permute-start(f32[16,1,512]{2,1,0:T(1,128)S(1)} %get-tuple-element.169), channel_id=1, source_target_pairs={{0,32},{32,64},{64,96},{96,128},{128,160},{160,192},{192,224},{224... | collective-permute-start | bytes 98312 | tf_op jit(solution)/shard_map/ppermute | solution.py:15
  3.2 5.2 %collective-permute-start.1 = (f32[16,1,512]{2,1,0:T(1,128)S(1)}, f32[16,1,512]{2,1,0:T(1,128)S(1)}, u32[]{:S(2)}, u32[]{:S(2)}) collective-permute-start(f32[16,1,512]{2,1,0:T(1,128)S(1)} %get-tuple-element.170), channel_id=1, source_target_pairs={{32,0},{64,32},{96,64},{128,96},{160,128},{192,160},{224,192},{256... | collective-permute-start | bytes 98312 | tf_op jit(solution)/shard_map/ppermute | solution.py:18
  9.4 7.0 %collective-permute-start.2 = (f32[1,66,512]{2,1,0:T(8,128)S(1)}, f32[1,66,512]{2,1,0:T(8,128)S(1)}, u32[]{:S(2)}, u32[]{:S(2)}) collective-permute-start(f32[1,66,512]{2,1,0:T(8,128)S(1)} %get-tuple-element.167), channel_id=1, source_target_pairs={{0,1},{1,2},{2,3},{3,4},{4,5},{5,6},{6,7},{7,8},{8,9},{9,10},{10,1... | collective-permute-start | bytes 405512 | tf_op jit(solution)/shard_map/ppermute | solution.py:15
  12.8 8.3 %collective-permute-start.3 = (f32[1,66,512]{2,1,0:T(8,128)S(1)}, f32[1,66,512]{2,1,0:T(8,128)S(1)}, u32[]{:S(2)}, u32[]{:S(2)}) collective-permute-start(f32[1,66,512]{2,1,0:T(8,128)S(1)} %get-tuple-element.168), channel_id=1, source_target_pairs={{1,0},{2,1},{3,2},{4,3},{5,4},{6,5},{7,6},{8,7},{9,8},{10,9},{11,1... | collective-permute-start | bytes 405512 | tf_op jit(solution)/shard_map/ppermute | solution.py:18
  178.5 10.3 %collective-permute-start.4 = (f32[4,16384]{1,0:T(4,128)S(1)}, f32[4,16384]{1,0:T(4,128)S(1)}, u32[]{:S(2)}, u32[]{:S(2)}) collective-permute-start(f32[4,16384]{1,0:T(4,128)S(1)} %get-tuple-element.165), channel_id=1, source_target_pairs={{0,1},{1,0},{2,3},{3,2},{4,5},{5,4},{6,7},{7,6},{8,9},{9,8},{10,11... | collective-permute-start | bytes 786440 | tf_op jit(solution)/shard_map/ppermute | solution.py:26
  189.0 34.9 %copy-start.2 = (s32[32]{0:T(128)S(1)}, s32[32]{0:T(128)}, u32[]{:S(2)}) copy-start(s32[32]{0:T(128)} %constant.176) | copy-start | bytes 388
  189.4 10.6 %collective-permute-start.5 = (f32[4,8192]{1,0:T(4,128)S(1)}, f32[4,8192]{1,0:T(4,128)S(1)}, u32[]{:S(2)}, u32[]{:S(2)}) collective-permute-start(f32[4,8192]{1,0:T(4,128)S(1)} %get-tuple-element.163), channel_id=1, source_target_pairs={{0,2},{1,3},{2,0},{3,1},{4,6},{5,7},{6,4},{7,5},{8,10},{9,11},{10,... | collective-permute-start | bytes 393224 | tf_op jit(solution)/shard_map/ppermute | solution.py:26
  200.3 6.5 %collective-permute-start.6 = (f32[4,4096]{1,0:T(4,128)S(1)}, f32[4,4096]{1,0:T(4,128)S(1)}, u32[]{:S(2)}, u32[]{:S(2)}) collective-permute-start(f32[4,4096]{1,0:T(4,128)S(1)} %get-tuple-element.161), channel_id=1, source_target_pairs={{0,4},{1,5},{2,6},{3,7},{4,0},{5,1},{6,2},{7,3},{8,12},{9,13},{10,... | collective-permute-start | bytes 196616 | tf_op jit(solution)/shard_map/ppermute | solution.py:26
  207.0 10.4 %collective-permute-start.7 = (f32[4,2048]{1,0:T(4,128)S(1)}, f32[4,2048]{1,0:T(4,128)S(1)}, u32[]{:S(2)}, u32[]{:S(2)}) collective-permute-start(f32[4,2048]{1,0:T(4,128)S(1)} %get-tuple-element.159), channel_id=1, source_target_pairs={{0,8},{1,9},{2,10},{3,11},{4,12},{5,13},{6,14},{7,15},{8,0},{9,1},... | collective-permute-start | bytes 98312 | tf_op jit(solution)/shard_map/ppermute | solution.py:26
  217.5 9.5 %collective-permute-start.8 = (f32[4,1024]{1,0:T(4,128)S(1)}, f32[4,1024]{1,0:T(4,128)S(1)}, u32[]{:S(2)}, u32[]{:S(2)}) collective-permute-start(f32[4,1024]{1,0:T(4,128)S(1)} %get-tuple-element.157), channel_id=1, source_target_pairs={{0,16},{1,17},{2,18},{3,19},{4,20},{5,21},{6,22},{7,23},{8,24},{9,... | collective-permute-start | bytes 49160 | tf_op jit(solution)/shard_map/ppermute | solution.py:26
where the time goes:
time: 283 us; the launch traced here: 281 us
  local copies, waits for them, and re-layouts  62.1 us (22%)
  blocking collectives  51.1 us (18%)
  loops' own time  47 us (17%)
  starting transfers between devices  40.1 us (14%)
  other arithmetic  32.8 us (12%)
  waiting for transfers between devices  25 us (9%)
  matrix products  22.1 us (8%)
    all_gather x1, blocking collectives, local(): collected = lax.all_gather(image_part, 'slab', axis=1, tiled=True)  51.1 us
    another operation x1, loops' own time, local(): lax.scan(advance, start_totals, jnp.arange(block_count, dtype=jnp.int32))  47 us
    ppermute x5, starting transfers between devices, swapped(): return lax.ppermute(value, axis, pairs)  29.9 us
    mul x16, other arithmetic, optics(): return (passing, weight[None] * looked[:3])  21.7 us
    dot_general x16, matrix products, advance(): jnp.dot(arc_params, one_hot, preferred_element_type=jnp.float32)  21.4 us
    slice x16, local copies, waits for them, and re-layouts, optics(): looked[4]  17.3 us
    ppermute x5, waiting for transfers between devices, swapped(): return lax.ppermute(value, axis, pairs)  17.3 us
    while x32, local copies, waits for them, and re-layouts  15.3 us
  transfers between devices with their start and end apart: 9, of which 8 were waited for; matrix products, arithmetic and copies ran while one was open for 0% of the time, Pallas kernels for 0%

commit v1 on v0

v1 whole, which is shorter than its diff:
```python
import functools
import math

import jax
import jax.numpy as jnp
from jax import lax
from jax.experimental import pallas as pl
from jax.experimental.pallas import tpu as pltpu
from jax.sharding import PartitionSpec as P

LOG2E = math.log2(math.e)
SUB = 8
LANE = 128


def gathered(table, index):
    return jnp.take_along_axis(table, index, axis=1, mode="promise_in_bounds")


def fill_tables(arc_tf_ref, tf_ref, raw, arcs, tables, step_len):
    rows, tf_count = tf_ref.shape
    raw[...] = jnp.zeros_like(raw)
    raw[0:rows, 0:tf_count] = tf_ref[...].astype(jnp.float32)
    arcs[...] = jnp.zeros_like(arcs)
    arcs[0:1, 0 : arc_tf_ref.shape[1]] = arc_tf_ref[...]
    index = jnp.broadcast_to(arcs[0:1, :], (SUB, LANE))
    looked = [
        gathered(jnp.broadcast_to(raw[j : j + 1, :], (SUB, LANE)), index) for j in range(rows)
    ]
    for c in range(3):
        tables[c] = looked[c]
    tables[3] = looked[3] * (-step_len * LOG2E)
    tables[4] = looked[4]
    tables[5] = looked[5] * looked[5] * (-LOG2E)


def cast_kernel(
    step_len, field, ids, front, back, above, below, arc_tf, tf, part, vol, arc, raw, arcs, tables, sems
):
    depth, rows, columns = field.shape
    bands, strips = rows // SUB, columns // LANE

    def copies(band):
        span = pl.ds(band * SUB, SUB)
        return [
            pltpu.make_async_copy(
                field.at[:, span, :], vol.at[pl.ds(1, depth), span, :], sems.at[0, band]
            ),
            pltpu.make_async_copy(ids.at[:, span, :], arc.at[:, span, :], sems.at[1, band]),
        ]

    for band in range(bands):
        for copy in copies(band):
            copy.start()
    vol[0:1] = front[...]
    vol[depth + 1 : depth + 2] = back[...]
    fill_tables(arc_tf, tf, raw, arcs, tables, step_len)
    lane = lax.broadcasted_iota(jnp.int32, (SUB, LANE), 1)
    row = lax.broadcasted_iota(jnp.int32, (SUB, LANE), 0)
    first_lane, last_lane = lane == 0, lane == LANE - 1
    first_row, last_row = row == 0, row == SUB - 1
    zero = jnp.zeros((SUB, LANE), jnp.float32)

    for copy in copies(0):
        copy.wait()
    for band in range(bands):
        if band + 1 < bands:
            for copy in copies(band + 1):
                copy.wait()
        top = band * SUB

        def layer(z, totals, band=band, top=top):
            center = [vol[z + 1, top : top + SUB, s * LANE : (s + 1) * LANE] for s in range(strips)]
            to_right = [pltpu.roll(c, 1, 1) for c in center]
            to_left = [pltpu.roll(c, LANE - 1, 1) for c in center]
            out = []
            for s in range(strips):
                cols = slice(s * LANE, (s + 1) * LANE)
                c = center[s]
                left = jnp.where(first_lane, to_right[s - 1] if s else zero, to_right[s])
                right = jnp.where(last_lane, to_left[s + 1] if s + 1 < strips else zero, to_left[s])
                if band == 0:
                    over = above[z, 0:1, cols]
                else:
                    over = vol[z + 1, top - 1 : top, cols]
                if band == bands - 1:
                    under = below[z, 0:1, cols]
                else:
                    under = vol[z + 1, top + SUB : top + SUB + 1, cols]
                up = jnp.where(first_row, over, pltpu.roll(c, 1, 0))
                down = jnp.where(last_row, under, pltpu.roll(c, SUB - 1, 0))
                dx = right - left
                dy = down - up
                dz = vol[z + 2, top : top + SUB, cols] - vol[z, top : top + SUB, cols]
                slant = jnp.abs(0.312 * dx + 0.39 * dy + 0.416 * dz)
                shading = 0.35 + slant * lax.rsqrt(4.0 + dx * dx + dy * dy + dz * dz)
                index = arc[z, top : top + SUB, cols]
                looked = [gathered(tables[j], index) for j in range(6)]
                off = c - looked[4]
                passing = jnp.exp2(looked[3] * jnp.exp2(off * off * looked[5]))
                red, green, blue, transmit = totals[s]
                after = transmit * passing
                weight = (transmit - after) * shading
                out.append(
                    (
                        red + weight * looked[0],
                        green + weight * looked[1],
                        blue + weight * looked[2],
                        after,
                    )
                )
            return tuple(out)

        start = tuple((zero, zero, zero, zero + 1.0) for _ in range(strips))
        totals = lax.fori_loop(0, depth, layer, start, unroll=2)
        for s in range(strips):
            for j in range(4):
                part[band * strips + s, j] = totals[s][j]


def merge_kernel(parts, out):
    count = parts.shape[0]
    red, green, blue, transmit = (parts[0, j] for j in range(4))
    for s in range(1, count):
        red = red + transmit * parts[s, 0]
        green = green + transmit * parts[s, 1]
        blue = blue + transmit * parts[s, 2]
        transmit = transmit * parts[s, 3]
    for s in range(count):
        for j, value in enumerate((red, green, blue, 1.0 - transmit)):
            out[s, j] = value


def shifted(value, axis, step):
    count = lax.axis_size(axis)
    return lax.ppermute(
        value, axis, [(i, i + step) for i in range(count) if 0 <= i + step < count]
    )


def local(field, arc_ids, arc_tf, tf_table):
    depth, rows, columns = field.shape
    slabs = lax.axis_size("slab")
    bands, strips = rows // SUB, columns // LANE
    above = shifted(field[:, rows - 1 :, :], "tile", 1)
    below = shifted(field[:, :1, :], "tile", -1)
    front = shifted(field[depth - 1 :], "slab", 1)
    back = shifted(field[:1], "slab", -1)
    vmem = pl.BlockSpec(memory_space=pltpu.VMEM)
    hbm = pl.BlockSpec(memory_space=pl.ANY)
    parts = pl.pallas_call(
        functools.partial(cast_kernel, 2.0 / (depth * slabs)),
        out_shape=jax.ShapeDtypeStruct((bands * strips, 4, SUB, LANE), jnp.float32),
        in_specs=[hbm, hbm] + [vmem] * 6,
        out_specs=vmem,
        scratch_shapes=[
            pltpu.VMEM((depth + 2, rows, columns), jnp.float32),
            pltpu.VMEM((depth, rows, columns), jnp.int32),
            pltpu.VMEM((SUB, LANE), jnp.float32),
            pltpu.VMEM((SUB, LANE), jnp.int32),
            pltpu.VMEM((6, SUB, LANE), jnp.float32),
            pltpu.SemaphoreType.DMA((2, bands)),
        ],
        compiler_params=pltpu.CompilerParams(vmem_limit_bytes=16 * 2**20),
        name="cast",
    )(field, arc_ids, front, back, above, below, arc_tf[None, :], tf_table)
    received = lax.all_to_all(parts, "slab", 0, 0, tiled=True)
    merged = pl.pallas_call(
        merge_kernel,
        out_shape=jax.ShapeDtypeStruct((slabs, 4, SUB, LANE), jnp.float32),
        in_specs=[vmem],
        out_specs=vmem,
        name="merge",
    )(received)
    pixels = lax.all_to_all(merged, "slab", 0, 0, tiled=True)
    pixels = pixels.reshape(bands, strips, 4, SUB, LANE).transpose(2, 0, 3, 1, 4)
    return pixels.reshape(4, rows, columns)


def solution(mesh):
    in_specs = (P("slab", "tile", None), P("slab", "tile", None), P(), P())
    out_specs = P(None, "tile", None)
    return jax.shard_map(local, mesh=mesh, in_specs=in_specs, out_specs=out_specs, check_vma=False)
```

time: 283 us -> 90.6 us (0.32)
  the two profiles are of different devices: /device:TPU:8 before, /device:TPU:24 now
where the time goes in v1:
time: 90.6 us; the launch traced here: 90.2 us
  blocking collectives  55.3 us (61%)
  Pallas kernels  14.3 us (16%)
  starting transfers between devices  10.2 us (11%)
  local copies, waits for them, and re-layouts  7.44 us (8%)
  waiting for transfers between devices  2.82 us (3%)
    all_to_all x1, blocking collectives, local(): received = lax.all_to_all(parts, 'slab', 0, 0, tiled=True)  33.4 us
    all_to_all x1, blocking collectives, local(): pixels = lax.all_to_all(merged, 'slab', 0, 0, tiled=True)  21.9 us
    pallas_call x1, Pallas kernels, local(): pl.pallas_call(functools.partial(cast_kernel, 2.0 / (depth * slabs)), out...  12.4 us
    ppermute x4, starting transfers between devices, shifted(): lax.ppermute(value, axis, [(i, i + step) for i in range(count) if 0 <= i...  10.2 us
    unnamed x8, local copies, waits for them, and re-layouts  4.52 us
    ppermute x4, waiting for transfers between devices, shifted(): lax.ppermute(value, axis, [(i, i + step) for i in range(count) if 0 <= i...  2.82 us
    pallas_call x1, Pallas kernels, local(): pl.pallas_call(merge_kernel, out_shape=jax.ShapeDtypeStruct((slabs, 4, SU...  1.93 us
  transfers between devices with their start and end apart: 4, of which 1 were waited for; matrix products, arithmetic and copies ran while one was open for 1% of the time, Pallas kernels for 0%

profile of v1, /device:TPU:24, one launch (start us, length us, event | category | flops | bytes accessed | tf_op | source)
XLA Modules:
  0.0 90.2 jit_solution(12612381020411465841)
XLA Ops:
  0.0 1.0 %fusion.1 = (f32[1,64,512]{2,1,0:T(8,128)S(1)}, f32[1,64,512]{2,1,0:T(8,128)S(1)}) fusion(f32[16,64,512]{2,1,0:T(8,128)} %field.1), kind=kLoop, calls=%fused_computation.2 | loop fusion | bytes 524288 | tf_op jit(solution)/shard_map/slice | solution.py:148
  1.0 1.3 %collective-permute-start.1 = (f32[1,64,512]{2,1,0:T(8,128)S(1)}, f32[1,64,512]{2,1,0:T(8,128)S(1)}, u32[]{:S(2)}, u32[]{:S(2)}) collective-permute-start(f32[1,64,512]{2,1,0:T(8,128)S(1)} %get-tuple-element.7), channel_id=1, source_target_pairs={{1,0},{2,1},{3,2},{4,3},{5,4},{6,5},{7,6},{8,7},{9,8},{10,9},{11,1... | collective-permute-start | bytes 393224 | tf_op jit(solution)/shard_map/ppermute | solution.py:136
  2.3 4.6 %collective-permute-start = (f32[1,64,512]{2,1,0:T(8,128)S(1)}, f32[1,64,512]{2,1,0:T(8,128)S(1)}, u32[]{:S(2)}, u32[]{:S(2)}) collective-permute-start(f32[1,64,512]{2,1,0:T(8,128)S(1)} %get-tuple-element.8), channel_id=1, source_target_pairs={{0,1},{1,2},{2,3},{3,4},{4,5},{5,6},{6,7},{7,8},{8,9},{9,10},{10,1... | collective-permute-start | bytes 393224 | tf_op jit(solution)/shard_map/ppermute | solution.py:136
  6.9 1.1 %fusion = (f32[16,1,512]{2,1,0:T(1,128)S(1)}, f32[16,1,512]{2,1,0:T(1,128)S(1)}) fusion(f32[16,64,512]{2,1,0:T(8,128)} %field.1), kind=kLoop, calls=%fused_computation.1 | loop fusion | bytes 131072 | tf_op jit(solution)/shard_map/slice | solution.py:146
  7.9 1.9 %collective-permute-start.3 = (f32[16,1,512]{2,1,0:T(1,128)S(1)}, f32[16,1,512]{2,1,0:T(1,128)S(1)}, u32[]{:S(2)}, u32[]{:S(2)}) collective-permute-start(f32[16,1,512]{2,1,0:T(1,128)S(1)} %get-tuple-element.5), channel_id=1, source_target_pairs={{32,0},{64,32},{96,64},{128,96},{160,128},{192,160},{224,192},{256... | collective-permute-start | bytes 98312 | tf_op jit(solution)/shard_map/ppermute | solution.py:136
  9.9 2.4 %collective-permute-start.2 = (f32[16,1,512]{2,1,0:T(1,128)S(1)}, f32[16,1,512]{2,1,0:T(1,128)S(1)}, u32[]{:S(2)}, u32[]{:S(2)}) collective-permute-start(f32[16,1,512]{2,1,0:T(1,128)S(1)} %get-tuple-element.6), channel_id=1, source_target_pairs={{0,32},{32,64},{64,96},{96,128},{128,160},{160,192},{192,224},{224... | collective-permute-start | bytes 98312 | tf_op jit(solution)/shard_map/ppermute | solution.py:136
  12.3 0.0 collective-permute-done.3.below
  12.3 2.8 %collective-permute-done.2.above = f32[16,1,512]{2,1,0:T(1,128)S(1)} collective-permute-done((f32[16,1,512]{2,1,0:T(1,128)S(1)}, f32[16,1,512]{2,1,0:T(1,128)S(1)}, u32[]{:S(2)}, u32[]{:S(2)}) %collective-permute-start.2) | collective-permute-done | bytes 32800 | tf_op jit(solution)/shard_map/ppermute | solution.py:136
  15.1 0.0 collective-permute-done.1.back
  15.1 0.0 collective-permute-done.front
  15.1 0.0 copy-start
  15.1 1.6 %copy-done = f32[16,64,512]{2,1,0:T(8,128)S(1)} copy-done((f32[16,64,512]{2,1,0:T(8,128)S(1)}, f32[16,64,512]{2,1,0:T(8,128)}, u32[]{:S(2)}) %copy-start) | copy-done | bytes 2097176
  16.7 0.0 copy-start.1
  16.7 1.6 %copy-done.1 = s32[16,64,512]{2,1,0:T(8,128)S(1)} copy-done((s32[16,64,512]{2,1,0:T(8,128)S(1)}, s32[16,64,512]{2,1,0:T(8,128)}, u32[]{:S(2)}) %copy-start.1) | copy-done | bytes 2097176
  18.3 0.0 copy-start.2
  18.3 0.7 copy-done.2
  19.0 0.0 copy-start.3
  19.0 0.7 copy-done.3
  19.6 12.4 %cast.1 = f32[32,4,8,128]{3,2,1,0:T(8,128)S(1)} custom-call(f32[16,64,512]{2,1,0:T(8,128)S(1)} %copy-done, s32[16,64,512]{2,1,0:T(8,128)S(1)} %copy-done.1, f32[1,64,512]{2,1,0:T(8,128)S(1)} %collective-permute-done.front, f32[1,64,512]{2,1,0:T(8,128)S(1)} %collective-permute-done.1.back, f32[16,1,512]{2,1,0:T(1,128)S(1)} %collective-permute-done.2.above, ...), custom_call_target="tpu_custom_call" | custom-call | tf_op jit(solution)/shard_map/cast/pallas_call | solution.py:151
  32.0 33.4 %all_to_all.10.parts = f32[32,4,8,128]{3,2,1,0:T(8,128)} all-to-all(f32[32,4,8,128]{3,2,1,0:T(8,128)S(1)} %cast.1), channel_id=1, replica_groups=mesh['tile'=16,'slab'=32] {'slab'}, dimensions={0} | all-to-all | bytes 1048576 | tf_op jit(solution)/shard_map/all_to_all | solution.py:167
  65.5 1.9 %merge.1 = f32[32,4,8,128]{3,2,1,0:T(8,128)} custom-call(f32[32,4,8,128]{3,2,1,0:T(8,128)} %all_to_all.10.parts), custom_call_target="tpu_custom_call" | custom-call | tf_op jit(solution)/shard_map/merge/pallas_call | solution.py:168
  67.4 21.9 %all_to_all.11 = f32[32,4,8,128]{3,2,1,0:T(8,128)S(1)} all-to-all(f32[32,4,8,128]{3,2,1,0:T(8,128)} %merge.1), channel_id=1, replica_groups=mesh['tile'=16,'slab'=32] {'slab'}, dimensions={0} | all-to-all | bytes 1048576 | tf_op jit(solution)/shard_map/all_to_all | solution.py:175
  89.3 0.9 copy.7
Async XLA Ops:
  1.0 14.1 %collective-permute-start.1 = (f32[1,64,512]{2,1,0:T(8,128)S(1)}, f32[1,64,512]{2,1,0:T(8,128)S(1)}, u32[]{:S(2)}, u32[]{:S(2)}) collective-permute-start(f32[1,64,512]{2,1,0:T(8,128)S(1)} %get-tuple-element.7), channel_id=1, source_target_pairs={{1,0},{2,1},{3,2},{4,3},{5,4},{6,5},{7,6},{8,7},{9,8},{10,9},{11,1... | collective-permute-start | bytes 393224 | tf_op jit(solution)/shard_map/ppermute | solution.py:136
  2.3 12.8 %collective-permute-start = (f32[1,64,512]{2,1,0:T(8,128)S(1)}, f32[1,64,512]{2,1,0:T(8,128)S(1)}, u32[]{:S(2)}, u32[]{:S(2)}) collective-permute-start(f32[1,64,512]{2,1,0:T(8,128)S(1)} %get-tuple-element.8), channel_id=1, source_target_pairs={{0,1},{1,2},{2,3},{3,4},{4,5},{5,6},{6,7},{7,8},{8,9},{9,10},{10,1... | collective-permute-start | bytes 393224 | tf_op jit(solution)/shard_map/ppermute | solution.py:136
  7.9 4.3 %collective-permute-start.3 = (f32[16,1,512]{2,1,0:T(1,128)S(1)}, f32[16,1,512]{2,1,0:T(1,128)S(1)}, u32[]{:S(2)}, u32[]{:S(2)}) collective-permute-start(f32[16,1,512]{2,1,0:T(1,128)S(1)} %get-tuple-element.5), channel_id=1, source_target_pairs={{32,0},{64,32},{96,64},{128,96},{160,128},{192,160},{224,192},{256... | collective-permute-start | bytes 98312 | tf_op jit(solution)/shard_map/ppermute | solution.py:136
  9.9 5.2 %collective-permute-start.2 = (f32[16,1,512]{2,1,0:T(1,128)S(1)}, f32[16,1,512]{2,1,0:T(1,128)S(1)}, u32[]{:S(2)}, u32[]{:S(2)}) collective-permute-start(f32[16,1,512]{2,1,0:T(1,128)S(1)} %get-tuple-element.6), channel_id=1, source_target_pairs={{0,32},{32,64},{64,96},{96,128},{128,160},{160,192},{192,224},{224... | collective-permute-start | bytes 98312 | tf_op jit(solution)/shard_map/ppermute | solution.py:136
  15.1 1.6 %copy-start = (f32[16,64,512]{2,1,0:T(8,128)S(1)}, f32[16,64,512]{2,1,0:T(8,128)}, u32[]{:S(2)}) copy-start(f32[16,64,512]{2,1,0:T(8,128)} %field.1) | copy-start | bytes 6291460
  16.7 1.6 %copy-start.1 = (s32[16,64,512]{2,1,0:T(8,128)S(1)}, s32[16,64,512]{2,1,0:T(8,128)}, u32[]{:S(2)}) copy-start(s32[16,64,512]{2,1,0:T(8,128)} %ids.1) | copy-start | bytes 6291460
  18.3 0.7 copy-start.2
  19.0 0.7 copy-start.3

commit v2 on v1

v2 whole, which is shorter than its diff:
```python
import functools
import math

import jax
import jax.numpy as jnp
from jax import lax
from jax.experimental import pallas as pl
from jax.experimental.pallas import tpu as pltpu
from jax.sharding import PartitionSpec as P

LOG2E = math.log2(math.e)
SUB = 8
LANE = 128
ALONG_LANES = lax.GatherDimensionNumbers(
    offset_dims=(),
    collapsed_slice_dims=(1,),
    start_index_map=(1,),
    operand_batching_dims=(0,),
    start_indices_batching_dims=(0,),
)
FRACTION = 2.0**30
GREEN_TOP = 2**16 - 1
WIDTH_TOP = 2**10 - 1
FINE = 512.0
CENTRE_UNIT = 2.0**-29
EXTINCTION_SPAN = 2**13


def gathered(table, index):
    return lax.gather(
        table, index[:, :, None], ALONG_LANES, (1, 1), mode=lax.GatherScatterMode.PROMISE_IN_BOUNDS
    )


def whole(value):
    return jnp.floor(value + 0.5).astype(jnp.int32)


def word(high, low, low_span):
    return whole((high - low.astype(jnp.float32)) / low_span) * low_span + low


def fill_tables(arc_tf, tf, raw, arcs, words):
    rows, tf_count = tf.shape
    raw[...] = jnp.zeros_like(raw)
    raw[0:rows, 0:tf_count] = tf[...].astype(jnp.float32)
    arcs[...] = jnp.zeros_like(arcs)
    arcs[0:1, 0 : arc_tf.shape[1]] = arc_tf[...]
    index = jnp.broadcast_to(arcs[0:1, :], (SUB, LANE))
    red, green, blue, extinction, centre, width = [
        gathered(jnp.broadcast_to(raw[j : j + 1, :], (SUB, LANE)), index) for j in range(rows)
    ]
    words[0] = word(red * FRACTION, whole(green * GREEN_TOP), GREEN_TOP + 1)
    words[1] = word(blue * FRACTION, whole(width * FINE), WIDTH_TOP + 1)
    words[2] = word(
        centre / CENTRE_UNIT, EXTINCTION_SPAN - whole(extinction * FINE), EXTINCTION_SPAN
    )


def compose(step_len, vol, arc, words, top, layers, front, back, above, below, totals):
    depth, rows, columns = vol.shape
    strips = columns // LANE
    band = pl.ds(top, SUB)
    lane = lax.broadcasted_iota(jnp.int32, (SUB, LANE), 1)
    row = lax.broadcasted_iota(jnp.int32, (SUB, LANE), 0)
    first_lane, last_lane = lane == 0, lane == LANE - 1
    first_row, last_row = row == 0, row == SUB - 1
    zero = jnp.zeros((SUB, LANE), jnp.float32)
    log_step = math.log2(step_len * LOG2E / FINE)
    totals = list(totals)
    for z in layers:
        center = [vol[z, band, s * LANE : (s + 1) * LANE] for s in range(strips)]
        to_right = [pltpu.roll(c, 1, 1) for c in center]
        to_left = [pltpu.roll(c, LANE - 1, 1) for c in center]
        for s in range(strips):
            cols = slice(s * LANE, (s + 1) * LANE)
            c = center[s]
            index = arc[z, band, cols]
            red_green, blue_width, centre_ext = [gathered(words[j], index) for j in range(3)]
            off = c - centre_ext.astype(jnp.float32) * CENTRE_UNIT
            reach = off * (blue_width & WIDTH_TOP).astype(jnp.float32)
            bell = jnp.exp2(reach * reach * (-LOG2E / FINE**2) + log_step)
            passing = jnp.exp2((centre_ext | -EXTINCTION_SPAN).astype(jnp.float32) * bell)

            left = jnp.where(first_lane, to_right[s - 1] if s else zero, to_right[s])
            right = jnp.where(last_lane, to_left[s + 1] if s + 1 < strips else zero, to_left[s])
            over = above[z, 0:1, cols] if above is not None else vol[z, pl.ds(top - SUB, SUB), cols]
            under = below[z, 0:1, cols] if below is not None else vol[z, pl.ds(top + SUB, SUB), cols]
            up = pltpu.roll(jnp.where(last_row, over, c), 1, 0)
            down = pltpu.roll(jnp.where(first_row, under, c), SUB - 1, 0)
            nearer = vol[z - 1, band, cols] if z else front[0, band, cols]
            farther = vol[z + 1, band, cols] if z + 1 < depth else back[0, band, cols]
            dx = right - left
            dy = down - up
            dz = farther - nearer
            slant = jnp.abs(0.312 * dx + 0.39 * dy + 0.416 * dz)
            shading = 0.35 + slant * lax.rsqrt(4.0 + dx * dx + dy * dy + dz * dz)

            red, green, blue, transmit = totals[s]
            after = transmit * passing
            weight = (transmit - after) * shading
            totals[s] = (
                red + weight * red_green.astype(jnp.float32),
                green + weight * (red_green & GREEN_TOP).astype(jnp.float32),
                blue + weight * blue_width.astype(jnp.float32),
                after,
            )
    return totals


def clear(strips):
    zero = jnp.zeros((SUB, LANE), jnp.float32)
    return [(zero, zero, zero, zero + 1.0)] * strips


def faces_kernel(field, first, last, top, bottom, top_band, bottom_band, sems):
    depth, rows, columns = field.shape
    copies = [
        pltpu.make_async_copy(field.at[depth - 1 :], last, sems.at[0]),
        pltpu.make_async_copy(field.at[:1], first, sems.at[1]),
        pltpu.make_async_copy(field.at[:, rows - SUB :, :], bottom_band, sems.at[2]),
        pltpu.make_async_copy(field.at[:, :SUB, :], top_band, sems.at[3]),
    ]
    for copy in copies:
        copy.start()
    for copy in copies:
        copy.wait()
    top[...] = top_band[:, 0:1, :]
    bottom[...] = bottom_band[:, SUB - 1 :, :]


def cast_kernel(
    step_len,
    field,
    ids,
    arc_tf,
    tf,
    front,
    back,
    above,
    below,
    parts,
    vol,
    arc,
    arc_tf_here,
    tf_here,
    raw,
    arcs,
    words,
    sems,
):
    depth, rows, columns = field.shape
    bands, strips = rows // SUB, columns // LANE

    def copies(band):
        span = pl.ds(pl.multiple_of(band * SUB, SUB), SUB)
        return [
            pltpu.make_async_copy(field.at[:, span, :], vol.at[:, span, :], sems.at[0, band]),
            pltpu.make_async_copy(ids.at[:, span, :], arc.at[:, span, :], sems.at[1, band]),
        ]

    small = [
        pltpu.make_async_copy(arc_tf, arc_tf_here, sems.at[2, 0]),
        pltpu.make_async_copy(tf, tf_here, sems.at[2, 1]),
    ]
    for copy in small:
        copy.start()
    for band in range(bands):
        for copy in copies(band):
            copy.start()
    for copy in small:
        copy.wait()
    fill_tables(arc_tf_here, tf_here, raw, arcs, words)
    slab, tile = lax.axis_index("slab"), lax.axis_index("tile")
    front[...] = front[...] * (slab > 0).astype(jnp.float32)
    back[...] = back[...] * (slab < lax.axis_size("slab") - 1).astype(jnp.float32)
    above[...] = above[...] * (tile > 0).astype(jnp.float32)
    below[...] = below[...] * (tile < lax.axis_size("tile") - 1).astype(jnp.float32)
    scale = (1.0 / FRACTION, 1.0 / GREEN_TOP, 1.0 / FRACTION, 1.0)

    def work(band, over, under):
        top = pl.multiple_of(band * SUB, SUB)
        totals = compose(
            step_len, vol, arc, words, top, range(depth), front, back, over, under, clear(strips)
        )
        for s in range(strips):
            for j in range(4):
                parts[band * strips + s, j] = totals[s][j] * scale[j]

    for copy in copies(0) + copies(1):
        copy.wait()
    work(0, above, None)

    def step(band, carry):
        for copy in copies(band + 1):
            copy.wait()
        work(band, None, None)
        return carry

    lax.fori_loop(1, bands - 1, step, 0)
    work(bands - 1, None, below)


def merge_kernel(parts, out):
    count = parts.shape[0]
    red, green, blue, transmit = (parts[0, j] for j in range(4))
    for s in range(1, count):
        red = red + transmit * parts[s, 0]
        green = green + transmit * parts[s, 1]
        blue = blue + transmit * parts[s, 2]
        transmit = transmit * parts[s, 3]
    for s in range(count):
        for j, value in enumerate((red, green, blue, 1.0 - transmit)):
            out[s, j] = value


def shifted(value, axis, step):
    count = lax.axis_size(axis)
    if axis == "tile":
        return lax.ppermute(value, axis, [(i, (i + step) % count) for i in range(count)])
    return lax.ppermute(
        value, axis, [(i, i + step) for i in range(count) if 0 <= i + step < count]
    )


def local(field, arc_ids, arc_tf, tf_table):
    depth, rows, columns = field.shape
    slabs = lax.axis_size("slab")
    step_len = 2.0 / (depth * slabs)
    bands, strips = rows // SUB, columns // LANE
    f32 = jnp.float32
    vmem = pl.BlockSpec(memory_space=pltpu.VMEM)
    hbm = pl.BlockSpec(memory_space=pltpu.HBM)
    shape = jax.ShapeDtypeStruct
    band_shape = (depth, SUB, columns)
    first, last, top, bottom = pl.pallas_call(
        faces_kernel,
        out_shape=[shape((1, rows, columns), f32)] * 2 + [shape((depth, 1, columns), f32)] * 2,
        in_specs=[hbm],
        out_specs=[vmem] * 4,
        scratch_shapes=[pltpu.VMEM(band_shape, f32)] * 2 + [pltpu.SemaphoreType.DMA((4,))],
        compiler_params=pltpu.CompilerParams(vmem_limit_bytes=52 * 2**20),
        name="faces",
    )(field)
    front = shifted(last, "slab", 1)
    back = shifted(first, "slab", -1)
    above = shifted(bottom, "tile", 1)
    below = shifted(top, "tile", -1)
    parts = pl.pallas_call(
        functools.partial(cast_kernel, step_len),
        out_shape=shape((bands * strips, 4, SUB, LANE), f32),
        in_specs=[hbm] * 4 + [vmem] * 4,
        out_specs=vmem,
        scratch_shapes=[
            pltpu.VMEM(field.shape, f32),
            pltpu.VMEM(field.shape, jnp.int32),
            pltpu.VMEM((1, arc_tf.shape[0]), jnp.int32),
            pltpu.VMEM(tf_table.shape, tf_table.dtype),
            pltpu.VMEM((SUB, LANE), f32),
            pltpu.VMEM((SUB, LANE), jnp.int32),
            pltpu.VMEM((3, SUB, LANE), jnp.int32),
            pltpu.SemaphoreType.DMA((3, max(bands, 2))),
        ],
        compiler_params=pltpu.CompilerParams(vmem_limit_bytes=52 * 2**20),
        name="cast",
    )(field, arc_ids, arc_tf[None, :], tf_table, front, back, above, below)
    received = lax.all_to_all(parts, "slab", 0, 0, tiled=True)
    merged = pl.pallas_call(
        merge_kernel,
        out_shape=shape((slabs, 4, SUB, LANE), f32),
        in_specs=[vmem],
        out_specs=vmem,
        compiler_params=pltpu.CompilerParams(vmem_limit_bytes=4 * 2**20),
        name="merge",
    )(received)
    pixels = lax.all_to_all(merged, "slab", 0, 0, tiled=True)
    pixels = pixels.reshape(bands, strips, 4, SUB, LANE).transpose(2, 0, 3, 1, 4)
    return pixels.reshape(4, rows, columns)


def solution(mesh):
    in_specs = (P("slab", "tile", None), P("slab", "tile", None), P(), P())
    out_specs = P(None, "tile", None)
    return jax.shard_map(local, mesh=mesh, in_specs=in_specs, out_specs=out_specs, check_vma=False)
```

time: 90.6 us -> 75.7 us (0.84)
  local copies, waits for them, and re-layouts: 7.44 us -> 0.87 us
  Pallas kernels: 14.3 us -> 8.01 us
  starting transfers between devices: 10.2 us -> 6.45 us
  blocking collectives: 55.3 us -> 56.3 us
  waiting for transfers between devices: 2.82 us -> 3.8 us
    pallas_call x2 -> x3, Pallas kernels: 14.3 us -> 8.01 us  [the longest x1 6.69 us: local(): pl.pallas_call(functools.partial(cast_kernel, step_len), out_shape=shape(...]
    ppermute x4 -> x2, starting transfers between devices: 10.2 us -> 4.69 us  [shifted(): lax.ppermute(value, axis, [(i, i + step) for i in range(count) if 0 <= i...]
    unnamed x8 -> x4, local copies, waits for them, and re-layouts: 4.52 us -> 0.01 us
    slice x2 -> x0, local copies, waits for them, and re-layouts: 2.07 us -> none  [the longest x1 1.08 us: local(): below = shifted(field[:, :1, :], 'tile', -1)]
    ppermute x0 -> x2, waiting for transfers between devices: none -> 1.86 us  [shifted(): lax.ppermute(value, axis, [(i, (i + step) % count) for i in range(count)])]
    ppermute x0 -> x2, starting transfers between devices: none -> 1.75 us  [shifted(): lax.ppermute(value, axis, [(i, (i + step) % count) for i in range(count)])]
    all_to_all x1, blocking collectives: 21.9 us -> 23.3 us  [local(): pixels = lax.all_to_all(merged, 'slab', 0, 0, tiled=True)]
    ppermute x4 -> x2, waiting for transfers between devices: 2.82 us -> 1.95 us  [shifted(): lax.ppermute(value, axis, [(i, i + step) for i in range(count) if 0 <= i...]
  transfers between devices with their start and end apart: 4 -> 4, of which waited for: 1 -> 3; matrix products, arithmetic and copies ran while one was open for 1% -> 0% of each run, Pallas kernels for 0% -> 0%
where the time goes in v2:
time: 75.7 us; the launch traced here: 75.5 us
  blocking collectives  56.3 us (74%)
  Pallas kernels  8.01 us (11%)
  starting transfers between devices  6.45 us (9%)
  waiting for transfers between devices  3.8 us (5%)
  local copies, waits for them, and re-layouts  0.87 us (1%)
    all_to_all x1, blocking collectives, local(): received = lax.all_to_all(parts, 'slab', 0, 0, tiled=True)  33 us
    all_to_all x1, blocking collectives, local(): pixels = lax.all_to_all(merged, 'slab', 0, 0, tiled=True)  23.3 us
    pallas_call x1, Pallas kernels, local(): pl.pallas_call(functools.partial(cast_kernel, step_len), out_shape=shape(...  6.69 us
    ppermute x2, starting transfers between devices, shifted(): lax.ppermute(value, axis, [(i, i + step) for i in range(count) if 0 <= i...  4.69 us
    ppermute x2, waiting for transfers between devices, shifted(): lax.ppermute(value, axis, [(i, i + step) for i in range(count) if 0 <= i...  1.95 us
    ppermute x2, waiting for transfers between devices, shifted(): lax.ppermute(value, axis, [(i, (i + step) % count) for i in range(count)])  1.86 us
    ppermute x2, starting transfers between devices, shifted(): lax.ppermute(value, axis, [(i, (i + step) % count) for i in range(count)])  1.75 us
  transfers between devices with their start and end apart: 4, of which 3 were waited for; matrix products, arithmetic and copies ran while one was open for 0% of the time, Pallas kernels for 0%

profile of v2, /device:TPU:24, one launch (start us, length us, event | category | flops | bytes accessed | tf_op | source)
XLA Modules:
  0.0 75.5 jit_solution(2502047056087321231)
XLA Ops:
  0.0 0.0 copy-start
  0.0 0.0 copy-start.1
  0.0 1.2 %faces.1 = (f32[1,64,512]{2,1,0:T(8,128)S(1)}, f32[1,64,512]{2,1,0:T(8,128)S(1)}, f32[16,1,512]{2,1,0:T(1,128)S(1)}, f32[16,1,512]{2,1,0:T(1,128)S(1)}) custom-call(f32[16,64,512]{2,1,0:T(8,128)} %field.3), custom_call_target="tpu_custom_call" | custom-call | tf_op jit(solution)/shard_map/faces/pallas_call | solution.py:236
  1.2 3.4 %collective-permute-start = (f32[1,64,512]{2,1,0:T(8,128)S(1)}, f32[1,64,512]{2,1,0:T(8,128)S(1)}, u32[]{:S(2)}, u32[]{:S(2)}) collective-permute-start(f32[1,64,512]{2,1,0:T(8,128)S(1)} %get-tuple-element.9), channel_id=1, source_target_pairs={{0,1},{1,2},{2,3},{3,4},{4,5},{5,6},{6,7},{7,8},{8,9},{9,10},{10,1... | collective-permute-start | bytes 393224 | tf_op jit(solution)/shard_map/ppermute | solution.py:221
  4.7 1.3 %collective-permute-start.1 = (f32[1,64,512]{2,1,0:T(8,128)S(1)}, f32[1,64,512]{2,1,0:T(8,128)S(1)}, u32[]{:S(2)}, u32[]{:S(2)}) collective-permute-start(f32[1,64,512]{2,1,0:T(8,128)S(1)} %get-tuple-element.10), channel_id=1, source_target_pairs={{1,0},{2,1},{3,2},{4,3},{5,4},{6,5},{7,6},{8,7},{9,8},{10,9},{11,1... | collective-permute-start | bytes 393224 | tf_op jit(solution)/shard_map/ppermute | solution.py:221
  6.0 0.0 collective-permute-start.2
  6.0 1.7 %collective-permute-start.3 = (f32[16,1,512]{2,1,0:T(1,128)S(1)}, f32[16,1,512]{2,1,0:T(1,128)S(1)}, u32[]{:S(2)}, u32[]{:S(2)}) collective-permute-start(f32[16,1,512]{2,1,0:T(1,128)S(1)} %get-tuple-element.12), channel_id=1, source_target_pairs={{0,480},{32,0},{64,32},{96,64},{128,96},{160,128},{192,160},{224,1... | collective-permute-start | bytes 98312 | tf_op jit(solution)/shard_map/ppermute | solution.py:220
  7.7 1.6 %collective-permute-done.2.above = f32[16,1,512]{2,1,0:T(1,128)S(1)} collective-permute-done((f32[16,1,512]{2,1,0:T(1,128)S(1)}, f32[16,1,512]{2,1,0:T(1,128)S(1)}, u32[]{:S(2)}, u32[]{:S(2)}) %collective-permute-start.2) | collective-permute-done | bytes 32800 | tf_op jit(solution)/shard_map/ppermute | solution.py:220
  9.3 0.3 collective-permute-done.3.below
  9.6 0.0 collective-permute-done.front
  9.6 1.9 %collective-permute-done.1.back = f32[1,64,512]{2,1,0:T(8,128)S(1)} collective-permute-done((f32[1,64,512]{2,1,0:T(8,128)S(1)}, f32[1,64,512]{2,1,0:T(8,128)S(1)}, u32[]{:S(2)}, u32[]{:S(2)}) %collective-permute-start.1) | collective-permute-done | bytes 131104 | tf_op jit(solution)/shard_map/ppermute | solution.py:221
  11.5 0.0 copy-done
  11.5 0.0 copy-done.1
  11.5 6.7 %cast.1 = f32[32,4,8,128]{3,2,1,0:T(8,128)S(1)} custom-call(f32[16,64,512]{2,1,0:T(8,128)} %field.3, s32[16,64,512]{2,1,0:T(8,128)} %ids.1, s32[1,64]{1,0:T(1,128)S(1)} %bitcast.7, bf16[6,16]{1,0:T(8,128)(2,1)S(1)} %copy-done, f32[1,64,512]{2,1,0:T(8,128)S(1)} %collective-permute-done.front, f32[1,64,512]{2,1,0:T(8,128)S(1)} %collective-permute-done.1.back, ...), custom_call_target="tpu_custom_call" | custom-call | tf_op jit(solution)/shard_map/cast/pallas_call | solution.py:249
  18.2 33.0 %all_to_all.10.parts = f32[32,4,8,128]{3,2,1,0:T(8,128)S(1)} all-to-all(f32[32,4,8,128]{3,2,1,0:T(8,128)S(1)} %cast.1), channel_id=1, replica_groups=mesh['tile'=16,'slab'=32] {'slab'}, dimensions={0} | all-to-all | bytes 1048576 | tf_op jit(solution)/shard_map/all_to_all | solution.py:267
  51.2 0.1 merge.1
  51.3 23.3 %all_to_all.11 = f32[32,4,8,128]{3,2,1,0:T(8,128)S(1)} all-to-all(f32[32,4,8,128]{3,2,1,0:T(8,128)S(1)} %merge.1), channel_id=1, replica_groups=mesh['tile'=16,'slab'=32] {'slab'}, dimensions={0} | all-to-all | bytes 1048576 | tf_op jit(solution)/shard_map/all_to_all | solution.py:276
  74.6 0.9 %copy.7 = f32[4,8,8,4,128]{4,2,3,1,0:T(8,128)} copy(f32[4,8,8,4,128]{4,2,0,3,1:T(8,128)S(1)} %bitcast.8) | data formatting | bytes 1048576 | tf_op jit(solution)/shard_map/transpose | solution.py:277
Async XLA Ops:
  0.0 11.5 %copy-start = (bf16[6,16]{1,0:T(8,128)(2,1)S(1)}, bf16[6,16]{1,0:T(8,128)(2,1)}, u32[]{:S(2)}) copy-start(bf16[6,16]{1,0:T(8,128)(2,1)} %tf.1) | copy-start | bytes 580
  0.0 11.5 %copy-start.1 = (s32[64]{0:T(128)S(1)}, s32[64]{0:T(128)}, u32[]{:S(2)}) copy-start(s32[64]{0:T(128)} %param.6) | copy-start | bytes 772
  1.2 8.3 %collective-permute-start = (f32[1,64,512]{2,1,0:T(8,128)S(1)}, f32[1,64,512]{2,1,0:T(8,128)S(1)}, u32[]{:S(2)}, u32[]{:S(2)}) collective-permute-start(f32[1,64,512]{2,1,0:T(8,128)S(1)} %get-tuple-element.9), channel_id=1, source_target_pairs={{0,1},{1,2},{2,3},{3,4},{4,5},{5,6},{6,7},{7,8},{8,9},{9,10},{10,1... | collective-permute-start | bytes 393224 | tf_op jit(solution)/shard_map/ppermute | solution.py:221
  4.7 6.9 %collective-permute-start.1 = (f32[1,64,512]{2,1,0:T(8,128)S(1)}, f32[1,64,512]{2,1,0:T(8,128)S(1)}, u32[]{:S(2)}, u32[]{:S(2)}) collective-permute-start(f32[1,64,512]{2,1,0:T(8,128)S(1)} %get-tuple-element.10), channel_id=1, source_target_pairs={{1,0},{2,1},{3,2},{4,3},{5,4},{6,5},{7,6},{8,7},{9,8},{10,9},{11,1... | collective-permute-start | bytes 393224 | tf_op jit(solution)/shard_map/ppermute | solution.py:221
  6.0 3.4 %collective-permute-start.2 = (f32[16,1,512]{2,1,0:T(1,128)S(1)}, f32[16,1,512]{2,1,0:T(1,128)S(1)}, u32[]{:S(2)}, u32[]{:S(2)}) collective-permute-start(f32[16,1,512]{2,1,0:T(1,128)S(1)} %get-tuple-element.11), channel_id=1, source_target_pairs={{0,32},{32,64},{64,96},{96,128},{128,160},{160,192},{192,224},{224... | collective-permute-start | bytes 98312 | tf_op jit(solution)/shard_map/ppermute | solution.py:220
  6.0 3.6 %collective-permute-start.3 = (f32[16,1,512]{2,1,0:T(1,128)S(1)}, f32[16,1,512]{2,1,0:T(1,128)S(1)}, u32[]{:S(2)}, u32[]{:S(2)}) collective-permute-start(f32[16,1,512]{2,1,0:T(1,128)S(1)} %get-tuple-element.12), channel_id=1, source_target_pairs={{0,480},{32,0},{64,32},{96,64},{128,96},{160,128},{192,160},{224,1... | collective-permute-start | bytes 98312 | tf_op jit(solution)/shard_map/ppermute | solution.py:220

commit v3 on v2

--- a/solution.py
+++ b/solution.py
@@ -113,64 +113,35 @@
     return [(zero, zero, zero, zero + 1.0)] * strips
 
 
-def faces_kernel(field, first, last, top, bottom, top_band, bottom_band, sems):
+def faces_kernel(field, first, last, top, bottom):
     depth, rows, columns = field.shape
-    copies = [
-        pltpu.make_async_copy(field.at[depth - 1 :], last, sems.at[0]),
-        pltpu.make_async_copy(field.at[:1], first, sems.at[1]),
-        pltpu.make_async_copy(field.at[:, rows - SUB :, :], bottom_band, sems.at[2]),
-        pltpu.make_async_copy(field.at[:, :SUB, :], top_band, sems.at[3]),
-    ]
-    for copy in copies:
-        copy.start()
-    for copy in copies:
-        copy.wait()
-    top[...] = top_band[:, 0:1, :]
-    bottom[...] = bottom_band[:, SUB - 1 :, :]
-
-
-def cast_kernel(
-    step_len,
-    field,
-    ids,
-    arc_tf,
-    tf,
-    front,
-    back,
-    above,
-    below,
-    parts,
-    vol,
-    arc,
-    arc_tf_here,
-    tf_here,
-    raw,
-    arcs,
-    words,
-    sems,
-):
-    depth, rows, columns = field.shape
+    last[...] = field[depth - 1 :]
+    first[...] = field[:1]
+    top[...] = field[:, 0:1, :]
+    bottom[...] = field[:, rows - 1 :, :]
+
+
+def inner_kernel(step_len, vol, arc, arc_tf, tf, words, inner, raw, arcs):
+    depth, rows, columns = vol.shape
     bands, strips = rows // SUB, columns // LANE
-
-    def copies(band):
-        span = pl.ds(pl.multiple_of(band * SUB, SUB), SUB)
-        return [
-            pltpu.make_async_copy(field.at[:, span, :], vol.at[:, span, :], sems.at[0, band]),
-            pltpu.make_async_copy(ids.at[:, span, :], arc.at[:, span, :], sems.at[1, band]),
-        ]
-
-    small = [
-        pltpu.make_async_copy(arc_tf, arc_tf_here, sems.at[2, 0]),
-        pltpu.make_async_copy(tf, tf_here, sems.at[2, 1]),
-    ]
-    for copy in small:
-        copy.start()
-    for band in range(bands):
-        for copy in copies(band):
-            copy.start()
-    for copy in small:
-        copy.wait()
-    fill_tables(arc_tf_here, tf_here, raw, arcs, words)
+    fill_tables(arc_tf, tf, raw, arcs, words)
+
+    def step(band, carry):
+        top = pl.multiple_of(band * SUB, SUB)
+        totals = compose(
+            step_len, vol, arc, words, top, range(1, depth - 1), None, None, None, None, clear(strips)
+        )
+        for s in range(strips):
+            for j in range(4):
+                inner[(band - 1) * strips + s, j] = totals[s][j]
+        return carry
+
+    lax.fori_loop(1, bands - 1, step, 0, unroll=3 if (bands - 2) % 3 == 0 else 1)
+
+
+def outer_kernel(step_len, vol, arc, words, inner, front, back, above, below, parts):
+    depth, rows, columns = vol.shape
+    bands, strips = rows // SUB, columns // LANE
     slab, tile = lax.axis_index("slab"), lax.axis_index("tile")
     front[...] = front[...] * (slab > 0).astype(jnp.float32)
     back[...] = back[...] * (slab < lax.axis_size("slab") - 1).astype(jnp.float32)
@@ -178,27 +149,39 @@
     below[...] = below[...] * (tile < lax.axis_size("tile") - 1).astype(jnp.float32)
     scale = (1.0 / FRACTION, 1.0 / GREEN_TOP, 1.0 / FRACTION, 1.0)
 
-    def work(band, over, under):
-        top = pl.multiple_of(band * SUB, SUB)
-        totals = compose(
-            step_len, vol, arc, words, top, range(depth), front, back, over, under, clear(strips)
-        )
+    def put(band, totals):
         for s in range(strips):
             for j in range(4):
                 parts[band * strips + s, j] = totals[s][j] * scale[j]
 
-    for copy in copies(0) + copies(1):
-        copy.wait()
-    work(0, above, None)
+    def whole_band(band, over, under):
+        top = band * SUB
+        put(
+            band,
+            compose(
+                step_len, vol, arc, words, top, range(depth), front, back, over, under, clear(strips)
+            ),
+        )
 
     def step(band, carry):
-        for copy in copies(band + 1):
-            copy.wait()
-        work(band, None, None)
+        top = pl.multiple_of(band * SUB, SUB)
+        at = (step_len, vol, arc, words, top)
+        totals = compose(*at, [0], front, back, None, None, clear(strips))
+        for s in range(strips):
+            red, green, blue, transmit = totals[s]
+            behind = [inner[(band - 1) * strips + s, j] for j in range(4)]
+            totals[s] = (
+                red + transmit * behind[0],
+                green + transmit * behind[1],
+                blue + transmit * behind[2],
+                transmit * behind[3],
+            )
+        put(band, compose(*at, [depth - 1], front, back, None, None, totals))
         return carry
 
-    lax.fori_loop(1, bands - 1, step, 0)
-    work(bands - 1, None, below)
+    lax.fori_loop(1, bands - 1, step, 0, unroll=3 if (bands - 2) % 3 == 0 else 1)
+    whole_band(0, above, None)
+    whole_band(bands - 1, None, below)
 
 
 def merge_kernel(parts, out):
@@ -232,38 +215,41 @@
     vmem = pl.BlockSpec(memory_space=pltpu.VMEM)
     hbm = pl.BlockSpec(memory_space=pltpu.HBM)
     shape = jax.ShapeDtypeStruct
-    band_shape = (depth, SUB, columns)
     first, last, top, bottom = pl.pallas_call(
         faces_kernel,
         out_shape=[shape((1, rows, columns), f32)] * 2 + [shape((depth, 1, columns), f32)] * 2,
-        in_specs=[hbm],
+        in_specs=[vmem],
         out_specs=[vmem] * 4,
-        scratch_shapes=[pltpu.VMEM(band_shape, f32)] * 2 + [pltpu.SemaphoreType.DMA((4,))],
-        compiler_params=pltpu.CompilerParams(vmem_limit_bytes=52 * 2**20),
+        compiler_params=pltpu.CompilerParams(vmem_limit_bytes=40 * 2**20),
         name="faces",
     )(field)
     front = shifted(last, "slab", 1)
     back = shifted(first, "slab", -1)
     above = shifted(bottom, "tile", 1)
     below = shifted(top, "tile", -1)
+    words, inner = pl.pallas_call(
+        functools.partial(inner_kernel, step_len),
+        out_shape=[
+            shape((3, SUB, LANE), jnp.int32),
+            shape(((bands - 2) * strips, 4, SUB, LANE), f32),
+        ],
+        in_specs=[vmem] * 4,
+        out_specs=[vmem] * 2,
+        scratch_shapes=[pltpu.VMEM((SUB, LANE), f32), pltpu.VMEM((SUB, LANE), jnp.int32)],
+        compiler_params=pltpu.CompilerParams(vmem_limit_bytes=12 * 2**20),
+        cost_estimate=pl.CostEstimate(
+            flops=60 * field.size, bytes_accessed=8 * field.size, transcendentals=3 * field.size
+        ),
+        name="inner",
+    )(field, arc_ids, arc_tf[None, :], tf_table)
     parts = pl.pallas_call(
-        functools.partial(cast_kernel, step_len),
+        functools.partial(outer_kernel, step_len),
         out_shape=shape((bands * strips, 4, SUB, LANE), f32),
-        in_specs=[hbm] * 4 + [vmem] * 4,
+        in_specs=[vmem] * 8,
         out_specs=vmem,
-        scratch_shapes=[
-            pltpu.VMEM(field.shape, f32),
-            pltpu.VMEM(field.shape, jnp.int32),
-            pltpu.VMEM((1, arc_tf.shape[0]), jnp.int32),
-            pltpu.VMEM(tf_table.shape, tf_table.dtype),
-            pltpu.VMEM((SUB, LANE), f32),
-            pltpu.VMEM((SUB, LANE), jnp.int32),
-            pltpu.VMEM((3, SUB, LANE), jnp.int32),
-            pltpu.SemaphoreType.DMA((3, max(bands, 2))),
-        ],
-        compiler_params=pltpu.CompilerParams(vmem_limit_bytes=52 * 2**20),
-        name="cast",
-    )(field, arc_ids, arc_tf[None, :], tf_table, front, back, above, below)
+        compiler_params=pltpu.CompilerParams(vmem_limit_bytes=12 * 2**20),
+        name="outer",
+    )(field, arc_ids, words, inner, front, back, above, below)
     received = lax.all_to_all(parts, "slab", 0, 0, tiled=True)
     merged = pl.pallas_call(
         merge_kernel,

time: 75.7 us -> 71.4 us (0.943)
  waiting for transfers between devices: 3.8 us -> 0.54 us
  Pallas kernels: 8.01 us -> 5.17 us
  local copies, waits for them, and re-layouts: 0.87 us -> 2.46 us
    ppermute x2, waiting for transfers between devices: 1.86 us -> 0.01 us  [shifted(): lax.ppermute(value, axis, [(i, (i + step) % count) for i in range(count)])]
    pallas_call x1 -> x2, Pallas kernels: 6.69 us -> 5.05 us  [the longest x1 3.22 us: local(): pl.pallas_call(functools.partial(inner_kernel, step_len), out_shape=[shap...]
    unnamed x4 -> x8, local copies, waits for them, and re-layouts: 0.01 us -> 1.6 us
    ppermute x2, waiting for transfers between devices: 1.95 us -> 0.54 us  [shifted(): lax.ppermute(value, axis, [(i, i + step) for i in range(count) if 0 <= i...]
    pallas_call x1, Pallas kernels: 1.23 us -> 0.04 us  [local(): pl.pallas_call(faces_kernel, out_shape=[shape((1, rows, columns), f32)] *...]
  transfers between devices with their start and end apart: 4 -> 4, of which waited for: 3 -> 1; matrix products, arithmetic and copies ran while one was open for 0% -> 0% of each run, Pallas kernels for 0% -> 5%
where the time goes in v3:
time: 71.4 us; the launch traced here: 71.1 us
  blocking collectives  56.3 us (79%)
  starting transfers between devices  6.58 us (9%)
  Pallas kernels  5.17 us (7%)
  local copies, waits for them, and re-layouts  2.46 us (3%)
    all_to_all x1, blocking collectives, local(): received = lax.all_to_all(parts, 'slab', 0, 0, tiled=True)  33 us
    all_to_all x1, blocking collectives, local(): pixels = lax.all_to_all(merged, 'slab', 0, 0, tiled=True)  23.3 us
    ppermute x2, starting transfers between devices, shifted(): lax.ppermute(value, axis, [(i, i + step) for i in range(count) if 0 <= i...  4.83 us
    pallas_call x1, Pallas kernels, local(): pl.pallas_call(functools.partial(inner_kernel, step_len), out_shape=[shap...  3.22 us
    pallas_call x1, Pallas kernels, local(): pl.pallas_call(functools.partial(outer_kernel, step_len), out_shape=shape...  1.83 us
    ppermute x2, starting transfers between devices, shifted(): lax.ppermute(value, axis, [(i, (i + step) % count) for i in range(count)])  1.75 us
    unnamed x8, local copies, waits for them, and re-layouts  1.6 us
  transfers between devices with their start and end apart: 4, of which 1 were waited for; matrix products, arithmetic and copies ran while one was open for 0% of the time, Pallas kernels for 5%

profile of v3, /device:TPU:24, one launch (start us, length us, event | category | flops | bytes accessed | tf_op | source)
XLA Modules:
  0.0 71.1 jit_solution(3842072327599805173)
XLA Ops:
  0.0 0.0 copy-start
  0.0 1.6 %copy-done = f32[16,64,512]{2,1,0:T(8,128)S(1)} copy-done((f32[16,64,512]{2,1,0:T(8,128)S(1)}, f32[16,64,512]{2,1,0:T(8,128)}, u32[]{:S(2)}) %copy-start) | copy-done | bytes 2097176
  1.6 0.0 copy-start.1
  1.6 0.0 copy-start.2
  1.6 0.0 copy-start.3
  1.6 3.5 %collective-permute-start = (f32[1,64,512]{2,1,0:T(8,128)S(1)}, f32[1,64,512]{2,1,0:T(8,128)S(1)}, u32[]{:S(2)}, u32[]{:S(2)}) collective-permute-start(f32[1,64,512]{2,1,0:T(8,128)S(1)} %get-tuple-element.13), channel_id=1, source_target_pairs={{0,1},{1,2},{2,3},{3,4},{4,5},{5,6},{6,7},{7,8},{8,9},{9,10},{10,1... | collective-permute-start | bytes 393224 | tf_op jit(solution)/shard_map/ppermute | solution.py:204
  5.2 1.3 %collective-permute-start.1 = (f32[1,64,512]{2,1,0:T(8,128)S(1)}, f32[1,64,512]{2,1,0:T(8,128)S(1)}, u32[]{:S(2)}, u32[]{:S(2)}) collective-permute-start(f32[1,64,512]{2,1,0:T(8,128)S(1)} %get-tuple-element.14), channel_id=1, source_target_pairs={{1,0},{2,1},{3,2},{4,3},{5,4},{6,5},{7,6},{8,7},{9,8},{10,9},{11,1... | collective-permute-start | bytes 393224 | tf_op jit(solution)/shard_map/ppermute | solution.py:204
  6.5 0.0 collective-permute-start.2
  6.5 1.7 %collective-permute-start.3 = (f32[16,1,512]{2,1,0:T(1,128)S(1)}, f32[16,1,512]{2,1,0:T(1,128)S(1)}, u32[]{:S(2)}, u32[]{:S(2)}) collective-permute-start(f32[16,1,512]{2,1,0:T(1,128)S(1)} %get-tuple-element.16), channel_id=1, source_target_pairs={{0,480},{32,0},{64,32},{96,64},{128,96},{160,128},{192,160},{224,1... | collective-permute-start | bytes 98312 | tf_op jit(solution)/shard_map/ppermute | solution.py:203
  8.2 0.0 copy-done.1
  8.2 0.0 copy-done.2
  8.2 0.0 copy-done.3
  8.2 3.2 %inner.1 = (s32[3,8,128]{2,1,0:T(8,128)S(1)}, f32[24,4,8,128]{3,2,1,0:T(8,128)S(1)}) custom-call(f32[16,64,512]{2,1,0:T(8,128)S(1)} %copy-done, s32[16,64,512]{2,1,0:T(8,128)S(1)} %copy-done.1, s32[1,64]{1,0:T(1,128)S(1)} %bitcast.7, bf16[6,16]{1,0:T(8,128)(2,1)S(1)} %copy-done.2), custom_call_target="tpu_custom_call" | custom-call | flops 31457280 | bytes 4194304 | tf_op jit(solution)/shard_map/inner/pallas_call | solution.py:230
  11.5 0.0 collective-permute-done.2.above
  11.5 0.0 collective-permute-done.3.below
  11.5 0.0 collective-permute-done.front
  11.5 0.5 collective-permute-done.1.back
  12.0 1.8 %outer.1 = f32[32,4,8,128]{3,2,1,0:T(8,128)S(1)} custom-call(f32[16,64,512]{2,1,0:T(8,128)S(1)} %copy-done, s32[16,64,512]{2,1,0:T(8,128)S(1)} %copy-done.1, s32[3,8,128]{2,1,0:T(8,128)S(1)} %get-tuple-element.11.words, f32[24,4,8,128]{3,2,1,0:T(8,128)S(1)} %get-tuple-element.12.inner, f32[1,64,512]{2,1,0:T(8,128)S(1)} %collective-permute-done.front, ...), custom_call_target="tpu_custom_call" | custom-call | tf_op jit(solution)/shard_map/outer/pallas_call | solution.py:245
  13.9 33.0 %all_to_all.10.parts = f32[32,4,8,128]{3,2,1,0:T(8,128)S(1)} all-to-all(f32[32,4,8,128]{3,2,1,0:T(8,128)S(1)} %outer.1), channel_id=1, replica_groups=mesh['tile'=16,'slab'=32] {'slab'}, dimensions={0} | all-to-all | bytes 1048576 | tf_op jit(solution)/shard_map/all_to_all | solution.py:253
  46.9 0.1 merge.1
  47.0 23.3 %all_to_all.11 = f32[32,4,8,128]{3,2,1,0:T(8,128)S(1)} all-to-all(f32[32,4,8,128]{3,2,1,0:T(8,128)S(1)} %merge.1), channel_id=1, replica_groups=mesh['tile'=16,'slab'=32] {'slab'}, dimensions={0} | all-to-all | bytes 1048576 | tf_op jit(solution)/shard_map/all_to_all | solution.py:262
  70.3 0.9 %copy.7 = f32[4,8,8,4,128]{4,2,3,1,0:T(8,128)} copy(f32[4,8,8,4,128]{4,2,0,3,1:T(8,128)S(1)} %bitcast.8) | data formatting | bytes 1048576 | tf_op jit(solution)/shard_map/transpose | solution.py:263
  (1 shorter events, 0.0 us)
Async XLA Ops:
  0.0 1.6 %copy-start = (f32[16,64,512]{2,1,0:T(8,128)S(1)}, f32[16,64,512]{2,1,0:T(8,128)}, u32[]{:S(2)}) copy-start(f32[16,64,512]{2,1,0:T(8,128)} %vol.3) | copy-start | bytes 6291460
  1.6 6.6 %copy-start.1 = (s32[16,64,512]{2,1,0:T(8,128)S(1)}, s32[16,64,512]{2,1,0:T(8,128)}, u32[]{:S(2)}) copy-start(s32[16,64,512]{2,1,0:T(8,128)} %arc.3) | copy-start | bytes 6291460
  1.6 6.6 %copy-start.2 = (bf16[6,16]{1,0:T(8,128)(2,1)S(1)}, bf16[6,16]{1,0:T(8,128)(2,1)}, u32[]{:S(2)}) copy-start(bf16[6,16]{1,0:T(8,128)(2,1)} %tf.1) | copy-start | bytes 580
  1.6 6.6 %copy-start.3 = (s32[64]{0:T(128)S(1)}, s32[64]{0:T(128)}, u32[]{:S(2)}) copy-start(s32[64]{0:T(128)} %param.6) | copy-start | bytes 772
  1.6 9.9 %collective-permute-start = (f32[1,64,512]{2,1,0:T(8,128)S(1)}, f32[1,64,512]{2,1,0:T(8,128)S(1)}, u32[]{:S(2)}, u32[]{:S(2)}) collective-permute-start(f32[1,64,512]{2,1,0:T(8,128)S(1)} %get-tuple-element.13), channel_id=1, source_target_pairs={{0,1},{1,2},{2,3},{3,4},{4,5},{5,6},{6,7},{7,8},{8,9},{9,10},{10,1... | collective-permute-start | bytes 393224 | tf_op jit(solution)/shard_map/ppermute | solution.py:204
  5.2 6.9 %collective-permute-start.1 = (f32[1,64,512]{2,1,0:T(8,128)S(1)}, f32[1,64,512]{2,1,0:T(8,128)S(1)}, u32[]{:S(2)}, u32[]{:S(2)}) collective-permute-start(f32[1,64,512]{2,1,0:T(8,128)S(1)} %get-tuple-element.14), channel_id=1, source_target_pairs={{1,0},{2,1},{3,2},{4,3},{5,4},{6,5},{7,6},{8,7},{9,8},{10,9},{11,1... | collective-permute-start | bytes 393224 | tf_op jit(solution)/shard_map/ppermute | solution.py:204
  6.5 5.0 %collective-permute-start.2 = (f32[16,1,512]{2,1,0:T(1,128)S(1)}, f32[16,1,512]{2,1,0:T(1,128)S(1)}, u32[]{:S(2)}, u32[]{:S(2)}) collective-permute-start(f32[16,1,512]{2,1,0:T(1,128)S(1)} %get-tuple-element.15), channel_id=1, source_target_pairs={{0,32},{32,64},{64,96},{96,128},{128,160},{160,192},{192,224},{224... | collective-permute-start | bytes 98312 | tf_op jit(solution)/shard_map/ppermute | solution.py:203
  6.5 5.0 %collective-permute-start.3 = (f32[16,1,512]{2,1,0:T(1,128)S(1)}, f32[16,1,512]{2,1,0:T(1,128)S(1)}, u32[]{:S(2)}, u32[]{:S(2)}) collective-permute-start(f32[16,1,512]{2,1,0:T(1,128)S(1)} %get-tuple-element.16), channel_id=1, source_target_pairs={{0,480},{32,0},{64,32},{96,64},{128,96},{160,128},{192,160},{224,1... | collective-permute-start | bytes 98312 | tf_op jit(solution)/shard_map/ppermute | solution.py:203

commit v4 on v3

--- a/solution.py
+++ b/solution.py
@@ -113,10 +113,11 @@
     return [(zero, zero, zero, zero + 1.0)] * strips
 
 
-def faces_kernel(field, first, last, top, bottom):
+def faces_kernel(field, layer_1, layer_2, top, bottom):
     depth, rows, columns = field.shape
-    last[...] = field[depth - 1 :]
-    first[...] = field[:1]
+    slab_odd = lax.axis_index("slab") % 2
+    layer_1[...] = field[pl.ds((1 - slab_odd) * (depth - 1), 1)]
+    layer_2[...] = field[pl.ds(slab_odd * (depth - 1), 1)]
     top[...] = field[:, 0:1, :]
     bottom[...] = field[:, rows - 1 :, :]
 
@@ -139,12 +140,15 @@
     lax.fori_loop(1, bands - 1, step, 0, unroll=3 if (bands - 2) % 3 == 0 else 1)
 
 
-def outer_kernel(step_len, vol, arc, words, inner, front, back, above, below, parts):
+def outer_kernel(step_len, vol, arc, words, inner, layer_1, layer_2, above, below, parts, halo):
     depth, rows, columns = vol.shape
     bands, strips = rows // SUB, columns // LANE
     slab, tile = lax.axis_index("slab"), lax.axis_index("tile")
-    front[...] = front[...] * (slab > 0).astype(jnp.float32)
-    back[...] = back[...] * (slab < lax.axis_size("slab") - 1).astype(jnp.float32)
+    slab_odd = slab % 2
+    slab_inner = (slab > 0) & (slab < lax.axis_size("slab") - 1)
+    halo[pl.ds(1 - slab_odd, 1)] = layer_1[...]
+    halo[pl.ds(slab_odd, 1)] = layer_2[...] * slab_inner.astype(jnp.float32)
+    front, back = halo.at[0:1], halo.at[1:2]
     above[...] = above[...] * (tile > 0).astype(jnp.float32)
     below[...] = below[...] * (tile < lax.axis_size("tile") - 1).astype(jnp.float32)
     scale = (1.0 / FRACTION, 1.0 / GREEN_TOP, 1.0 / FRACTION, 1.0)
@@ -206,6 +210,14 @@
     )
 
 
+def swapped(value, axis, first):
+    count = lax.axis_size(axis)
+    partner = {i: i for i in range(count)}
+    for i in range(first, count - 1, 2):
+        partner[i], partner[i + 1] = i + 1, i
+    return lax.ppermute(value, axis, list(partner.items()))
+
+
 def local(field, arc_ids, arc_tf, tf_table):
     depth, rows, columns = field.shape
     slabs = lax.axis_size("slab")
@@ -215,7 +227,7 @@
     vmem = pl.BlockSpec(memory_space=pltpu.VMEM)
     hbm = pl.BlockSpec(memory_space=pltpu.HBM)
     shape = jax.ShapeDtypeStruct
-    first, last, top, bottom = pl.pallas_call(
+    layer_1, layer_2, top, bottom = pl.pallas_call(
         faces_kernel,
         out_shape=[shape((1, rows, columns), f32)] * 2 + [shape((depth, 1, columns), f32)] * 2,
         in_specs=[vmem],
@@ -223,8 +235,8 @@
         compiler_params=pltpu.CompilerParams(vmem_limit_bytes=40 * 2**20),
         name="faces",
     )(field)
-    front = shifted(last, "slab", 1)
-    back = shifted(first, "slab", -1)
+    layer_2 = swapped(layer_2, "slab", 1)
+    layer_1 = swapped(layer_1, "slab", 0)
     above = shifted(bottom, "tile", 1)
     below = shifted(top, "tile", -1)
     words, inner = pl.pallas_call(
@@ -247,9 +259,10 @@
         out_shape=shape((bands * strips, 4, SUB, LANE), f32),
         in_specs=[vmem] * 8,
         out_specs=vmem,
+        scratch_shapes=[pltpu.VMEM((2, rows, columns), f32)],
         compiler_params=pltpu.CompilerParams(vmem_limit_bytes=12 * 2**20),
         name="outer",
-    )(field, arc_ids, words, inner, front, back, above, below)
+    )(field, arc_ids, words, inner, layer_1, layer_2, above, below)
     received = lax.all_to_all(parts, "slab", 0, 0, tiled=True)
     merged = pl.pallas_call(
         merge_kernel,

time: 71.4 us -> 70.1 us (0.982)
  transfers between devices with their start and end apart: 4 -> 4, of which waited for: 1 -> 0; matrix products, arithmetic and copies ran while one was open for 0% -> 0% of each run, Pallas kernels for 5% -> 5%
where the time goes in v4:
time: 70.1 us; the launch traced here: 69.8 us
  blocking collectives  56.2 us (80%)
  starting transfers between devices  5.95 us (8%)
  Pallas kernels  5.18 us (7%)
  local copies, waits for them, and re-layouts  2.46 us (4%)
    all_to_all x1, blocking collectives, local(): received = lax.all_to_all(parts, 'slab', 0, 0, tiled=True)  33 us
    all_to_all x1, blocking collectives, local(): pixels = lax.all_to_all(merged, 'slab', 0, 0, tiled=True)  23.1 us
    ppermute x2, starting transfers between devices, swapped(): return lax.ppermute(value, axis, list(partner.items()))  4.2 us
    pallas_call x1, Pallas kernels, local(): pl.pallas_call(functools.partial(inner_kernel, step_len), out_shape=[shap...  3.22 us
    pallas_call x1, Pallas kernels, local(): pl.pallas_call(functools.partial(outer_kernel, step_len), out_shape=shape...  1.84 us
    ppermute x2, starting transfers between devices, shifted(): lax.ppermute(value, axis, [(i, (i + step) % count) for i in range(count)])  1.75 us
    unnamed x8, local copies, waits for them, and re-layouts  1.6 us
  transfers between devices with their start and end apart: 4, of which 0 were waited for; matrix products, arithmetic and copies ran while one was open for 0% of the time, Pallas kernels for 5%

profile of v4, /device:TPU:24, one launch (start us, length us, event | category | flops | bytes accessed | tf_op | source)
XLA Modules:
  0.0 69.8 jit_solution(18185169727840466860)
XLA Ops:
  0.0 0.0 copy-start
  0.0 1.6 %copy-done = f32[16,64,512]{2,1,0:T(8,128)S(1)} copy-done((f32[16,64,512]{2,1,0:T(8,128)S(1)}, f32[16,64,512]{2,1,0:T(8,128)}, u32[]{:S(2)}) %copy-start) | copy-done | bytes 2097176
  1.6 0.0 copy-start.1
  1.6 0.0 copy-start.2
  1.6 0.0 copy-start.3
  1.6 3.5 %collective-permute-start = (f32[1,64,512]{2,1,0:T(8,128)S(1)}, f32[1,64,512]{2,1,0:T(8,128)S(1)}, u32[]{:S(2)}, u32[]{:S(2)}) collective-permute-start(f32[1,64,512]{2,1,0:T(8,128)S(1)} %get-tuple-element.13), channel_id=1, source_target_pairs={{0,1},{1,0},{2,3},{3,2},{4,5},{5,4},{6,7},{7,6},{8,9},{9,8},{10,11... | collective-permute-start | bytes 393224 | tf_op jit(solution)/shard_map/ppermute | solution.py:218
  5.2 0.7 collective-permute-start.1
  5.9 0.0 collective-permute-start.2
  5.9 1.7 %collective-permute-start.3 = (f32[16,1,512]{2,1,0:T(1,128)S(1)}, f32[16,1,512]{2,1,0:T(1,128)S(1)}, u32[]{:S(2)}, u32[]{:S(2)}) collective-permute-start(f32[16,1,512]{2,1,0:T(1,128)S(1)} %get-tuple-element.16), channel_id=1, source_target_pairs={{0,480},{32,0},{64,32},{96,64},{128,96},{160,128},{192,160},{224,1... | collective-permute-start | bytes 98312 | tf_op jit(solution)/shard_map/ppermute | solution.py:207
  7.6 0.0 copy-done.1
  7.6 0.0 copy-done.2
  7.6 0.0 copy-done.3
  7.6 3.2 %inner.1 = (s32[3,8,128]{2,1,0:T(8,128)S(1)}, f32[24,4,8,128]{3,2,1,0:T(8,128)S(1)}) custom-call(f32[16,64,512]{2,1,0:T(8,128)S(1)} %copy-done, s32[16,64,512]{2,1,0:T(8,128)S(1)} %copy-done.1, s32[1,64]{1,0:T(1,128)S(1)} %bitcast.7, bf16[6,16]{1,0:T(8,128)(2,1)S(1)} %copy-done.2), custom_call_target="tpu_custom_call" | custom-call | flops 31457280 | bytes 4194304 | tf_op jit(solution)/shard_map/inner/pallas_call | solution.py:242
  10.8 0.0 collective-permute-done.2.above
  10.9 0.0 collective-permute-done.3.below
  10.9 0.0 collective-permute-done.layer_1
  10.9 0.0 collective-permute-done.1.layer_2
  10.9 1.8 %outer.1 = f32[32,4,8,128]{3,2,1,0:T(8,128)S(1)} custom-call(f32[16,64,512]{2,1,0:T(8,128)S(1)} %copy-done, s32[16,64,512]{2,1,0:T(8,128)S(1)} %copy-done.1, s32[3,8,128]{2,1,0:T(8,128)S(1)} %get-tuple-element.11.words, f32[24,4,8,128]{3,2,1,0:T(8,128)S(1)} %get-tuple-element.12.inner, f32[1,64,512]{2,1,0:T(8,128)S(1)} %collective-permute-done.layer_1, ...), custom_call_target="tpu_custom_call" | custom-call | tf_op jit(solution)/shard_map/outer/pallas_call | solution.py:257
  12.7 33.0 %all_to_all.10.parts = f32[32,4,8,128]{3,2,1,0:T(8,128)S(1)} all-to-all(f32[32,4,8,128]{3,2,1,0:T(8,128)S(1)} %outer.1), channel_id=1, replica_groups=mesh['tile'=16,'slab'=32] {'slab'}, dimensions={0} | all-to-all | bytes 1048576 | tf_op jit(solution)/shard_map/all_to_all | solution.py:266
  45.8 0.1 merge.1
  45.9 23.1 %all_to_all.11 = f32[32,4,8,128]{3,2,1,0:T(8,128)S(1)} all-to-all(f32[32,4,8,128]{3,2,1,0:T(8,128)S(1)} %merge.1), channel_id=1, replica_groups=mesh['tile'=16,'slab'=32] {'slab'}, dimensions={0} | all-to-all | bytes 1048576 | tf_op jit(solution)/shard_map/all_to_all | solution.py:275
  69.0 0.9 %copy.7 = f32[4,8,8,4,128]{4,2,3,1,0:T(8,128)} copy(f32[4,8,8,4,128]{4,2,0,3,1:T(8,128)S(1)} %bitcast.8) | data formatting | bytes 1048576 | tf_op jit(solution)/shard_map/transpose | solution.py:276
  (1 shorter events, 0.0 us)
Async XLA Ops:
  0.0 1.6 %copy-start = (f32[16,64,512]{2,1,0:T(8,128)S(1)}, f32[16,64,512]{2,1,0:T(8,128)}, u32[]{:S(2)}) copy-start(f32[16,64,512]{2,1,0:T(8,128)} %vol.3) | copy-start | bytes 6291460
  1.6 6.0 %copy-start.1 = (s32[16,64,512]{2,1,0:T(8,128)S(1)}, s32[16,64,512]{2,1,0:T(8,128)}, u32[]{:S(2)}) copy-start(s32[16,64,512]{2,1,0:T(8,128)} %arc.3) | copy-start | bytes 6291460
  1.6 6.0 %copy-start.2 = (bf16[6,16]{1,0:T(8,128)(2,1)S(1)}, bf16[6,16]{1,0:T(8,128)(2,1)}, u32[]{:S(2)}) copy-start(bf16[6,16]{1,0:T(8,128)(2,1)} %tf.1) | copy-start | bytes 580
  1.6 6.0 %copy-start.3 = (s32[64]{0:T(128)S(1)}, s32[64]{0:T(128)}, u32[]{:S(2)}) copy-start(s32[64]{0:T(128)} %param.6) | copy-start | bytes 772
  1.6 9.2 %collective-permute-start = (f32[1,64,512]{2,1,0:T(8,128)S(1)}, f32[1,64,512]{2,1,0:T(8,128)S(1)}, u32[]{:S(2)}, u32[]{:S(2)}) collective-permute-start(f32[1,64,512]{2,1,0:T(8,128)S(1)} %get-tuple-element.13), channel_id=1, source_target_pairs={{0,1},{1,0},{2,3},{3,2},{4,5},{5,4},{6,7},{7,6},{8,9},{9,8},{10,11... | collective-permute-start | bytes 393224 | tf_op jit(solution)/shard_map/ppermute | solution.py:218
  5.2 5.7 %collective-permute-start.1 = (f32[1,64,512]{2,1,0:T(8,128)S(1)}, f32[1,64,512]{2,1,0:T(8,128)S(1)}, u32[]{:S(2)}, u32[]{:S(2)}) collective-permute-start(f32[1,64,512]{2,1,0:T(8,128)S(1)} %get-tuple-element.14), channel_id=1, source_target_pairs={{0,0},{1,2},{2,1},{3,4},{4,3},{5,6},{6,5},{7,8},{8,7},{9,10},{10,9... | collective-permute-start | bytes 393224 | tf_op jit(solution)/shard_map/ppermute | solution.py:218
  5.9 5.0 %collective-permute-start.2 = (f32[16,1,512]{2,1,0:T(1,128)S(1)}, f32[16,1,512]{2,1,0:T(1,128)S(1)}, u32[]{:S(2)}, u32[]{:S(2)}) collective-permute-start(f32[16,1,512]{2,1,0:T(1,128)S(1)} %get-tuple-element.15), channel_id=1, source_target_pairs={{0,32},{32,64},{64,96},{96,128},{128,160},{160,192},{192,224},{224... | collective-permute-start | bytes 98312 | tf_op jit(solution)/shard_map/ppermute | solution.py:207
  5.9 5.0 %collective-permute-start.3 = (f32[16,1,512]{2,1,0:T(1,128)S(1)}, f32[16,1,512]{2,1,0:T(1,128)S(1)}, u32[]{:S(2)}, u32[]{:S(2)}) collective-permute-start(f32[16,1,512]{2,1,0:T(1,128)S(1)} %get-tuple-element.16), channel_id=1, source_target_pairs={{0,480},{32,0},{64,32},{96,64},{128,96},{160,128},{192,160},{224,1... | collective-permute-start | bytes 98312 | tf_op jit(solution)/shard_map/ppermute | solution.py:207

commit v5 on v4

--- a/solution.py
+++ b/solution.py
@@ -183,7 +183,7 @@
         put(band, compose(*at, [depth - 1], front, back, None, None, totals))
         return carry
 
-    lax.fori_loop(1, bands - 1, step, 0, unroll=3 if (bands - 2) % 3 == 0 else 1)
+    lax.fori_loop(1, bands - 1, step, 0, unroll=True)
     whole_band(0, above, None)
     whole_band(bands - 1, None, below)
 

time: 70.1 us -> 69.9 us (level)
  no operation moved by 1% of the time
where the time goes in v5:
time: 69.9 us; the launch traced here: 69.6 us
  blocking collectives  56.2 us (80%)
  starting transfers between devices  5.95 us (9%)
  Pallas kernels  4.97 us (7%)
  local copies, waits for them, and re-layouts  2.46 us (4%)
    all_to_all x1, blocking collectives, local(): received = lax.all_to_all(parts, 'slab', 0, 0, tiled=True)  33 us
    all_to_all x1, blocking collectives, local(): pixels = lax.all_to_all(merged, 'slab', 0, 0, tiled=True)  23.1 us
    ppermute x2, starting transfers between devices, swapped(): return lax.ppermute(value, axis, list(partner.items()))  4.2 us
    pallas_call x1, Pallas kernels, local(): pl.pallas_call(functools.partial(inner_kernel, step_len), out_shape=[shap...  3.22 us
    ppermute x2, starting transfers between devices, shifted(): lax.ppermute(value, axis, [(i, (i + step) % count) for i in range(count)])  1.75 us
    pallas_call x1, Pallas kernels, local(): pl.pallas_call(functools.partial(outer_kernel, step_len), out_shape=shape...  1.63 us
    unnamed x8, local copies, waits for them, and re-layouts  1.6 us
  transfers between devices with their start and end apart: 4, of which 0 were waited for; matrix products, arithmetic and copies ran while one was open for 0% of the time, Pallas kernels for 5%

profile of v5, /device:TPU:24, one launch (start us, length us, event | category | flops | bytes accessed | tf_op | source)
XLA Modules:
  0.0 69.6 jit_solution(2820830508986571087)
XLA Ops:
  0.0 0.0 copy-start
  0.0 1.6 %copy-done = f32[16,64,512]{2,1,0:T(8,128)S(1)} copy-done((f32[16,64,512]{2,1,0:T(8,128)S(1)}, f32[16,64,512]{2,1,0:T(8,128)}, u32[]{:S(2)}) %copy-start) | copy-done | bytes 2097176
  1.6 0.0 copy-start.1
  1.6 0.0 copy-start.2
  1.6 0.0 copy-start.3
  1.6 3.5 %collective-permute-start = (f32[1,64,512]{2,1,0:T(8,128)S(1)}, f32[1,64,512]{2,1,0:T(8,128)S(1)}, u32[]{:S(2)}, u32[]{:S(2)}) collective-permute-start(f32[1,64,512]{2,1,0:T(8,128)S(1)} %get-tuple-element.13), channel_id=1, source_target_pairs={{0,1},{1,0},{2,3},{3,2},{4,5},{5,4},{6,7},{7,6},{8,9},{9,8},{10,11... | collective-permute-start | bytes 393224 | tf_op jit(solution)/shard_map/ppermute | solution.py:218
  5.2 0.7 collective-permute-start.1
  5.9 0.0 collective-permute-start.2
  5.9 1.7 %collective-permute-start.3 = (f32[16,1,512]{2,1,0:T(1,128)S(1)}, f32[16,1,512]{2,1,0:T(1,128)S(1)}, u32[]{:S(2)}, u32[]{:S(2)}) collective-permute-start(f32[16,1,512]{2,1,0:T(1,128)S(1)} %get-tuple-element.16), channel_id=1, source_target_pairs={{0,480},{32,0},{64,32},{96,64},{128,96},{160,128},{192,160},{224,1... | collective-permute-start | bytes 98312 | tf_op jit(solution)/shard_map/ppermute | solution.py:207
  7.6 0.0 copy-done.1
  7.6 0.0 copy-done.2
  7.6 0.0 copy-done.3
  7.6 3.2 %inner.1 = (s32[3,8,128]{2,1,0:T(8,128)S(1)}, f32[24,4,8,128]{3,2,1,0:T(8,128)S(1)}) custom-call(f32[16,64,512]{2,1,0:T(8,128)S(1)} %copy-done, s32[16,64,512]{2,1,0:T(8,128)S(1)} %copy-done.1, s32[1,64]{1,0:T(1,128)S(1)} %bitcast.7, bf16[6,16]{1,0:T(8,128)(2,1)S(1)} %copy-done.2), custom_call_target="tpu_custom_call" | custom-call | flops 31457280 | bytes 4194304 | tf_op jit(solution)/shard_map/inner/pallas_call | solution.py:242
  10.8 0.0 collective-permute-done.2.above
  10.9 0.0 collective-permute-done.3.below
  10.9 0.0 collective-permute-done.layer_1
  10.9 0.0 collective-permute-done.1.layer_2
  10.9 1.6 %outer.1 = f32[32,4,8,128]{3,2,1,0:T(8,128)S(1)} custom-call(f32[16,64,512]{2,1,0:T(8,128)S(1)} %copy-done, s32[16,64,512]{2,1,0:T(8,128)S(1)} %copy-done.1, s32[3,8,128]{2,1,0:T(8,128)S(1)} %get-tuple-element.11.words, f32[24,4,8,128]{3,2,1,0:T(8,128)S(1)} %get-tuple-element.12.inner, f32[1,64,512]{2,1,0:T(8,128)S(1)} %collective-permute-done.layer_1, ...), custom_call_target="tpu_custom_call" | custom-call | tf_op jit(solution)/shard_map/outer/pallas_call | solution.py:257
  12.5 33.0 %all_to_all.10.parts = f32[32,4,8,128]{3,2,1,0:T(8,128)S(1)} all-to-all(f32[32,4,8,128]{3,2,1,0:T(8,128)S(1)} %outer.1), channel_id=1, replica_groups=mesh['tile'=16,'slab'=32] {'slab'}, dimensions={0} | all-to-all | bytes 1048576 | tf_op jit(solution)/shard_map/all_to_all | solution.py:266
  45.6 0.1 merge.1
  45.6 23.1 %all_to_all.11 = f32[32,4,8,128]{3,2,1,0:T(8,128)S(1)} all-to-all(f32[32,4,8,128]{3,2,1,0:T(8,128)S(1)} %merge.1), channel_id=1, replica_groups=mesh['tile'=16,'slab'=32] {'slab'}, dimensions={0} | all-to-all | bytes 1048576 | tf_op jit(solution)/shard_map/all_to_all | solution.py:275
  68.8 0.9 %copy.7 = f32[4,8,8,4,128]{4,2,3,1,0:T(8,128)} copy(f32[4,8,8,4,128]{4,2,0,3,1:T(8,128)S(1)} %bitcast.8) | data formatting | bytes 1048576 | tf_op jit(solution)/shard_map/transpose | solution.py:276
  (1 shorter events, 0.0 us)
Async XLA Ops:
  0.0 1.6 %copy-start = (f32[16,64,512]{2,1,0:T(8,128)S(1)}, f32[16,64,512]{2,1,0:T(8,128)}, u32[]{:S(2)}) copy-start(f32[16,64,512]{2,1,0:T(8,128)} %vol.3) | copy-start | bytes 6291460
  1.6 6.0 %copy-start.1 = (s32[16,64,512]{2,1,0:T(8,128)S(1)}, s32[16,64,512]{2,1,0:T(8,128)}, u32[]{:S(2)}) copy-start(s32[16,64,512]{2,1,0:T(8,128)} %arc.3) | copy-start | bytes 6291460
  1.6 6.0 %copy-start.2 = (bf16[6,16]{1,0:T(8,128)(2,1)S(1)}, bf16[6,16]{1,0:T(8,128)(2,1)}, u32[]{:S(2)}) copy-start(bf16[6,16]{1,0:T(8,128)(2,1)} %tf.1) | copy-start | bytes 580
  1.6 6.0 %copy-start.3 = (s32[64]{0:T(128)S(1)}, s32[64]{0:T(128)}, u32[]{:S(2)}) copy-start(s32[64]{0:T(128)} %param.6) | copy-start | bytes 772
  1.6 9.2 %collective-permute-start = (f32[1,64,512]{2,1,0:T(8,128)S(1)}, f32[1,64,512]{2,1,0:T(8,128)S(1)}, u32[]{:S(2)}, u32[]{:S(2)}) collective-permute-start(f32[1,64,512]{2,1,0:T(8,128)S(1)} %get-tuple-element.13), channel_id=1, source_target_pairs={{0,1},{1,0},{2,3},{3,2},{4,5},{5,4},{6,7},{7,6},{8,9},{9,8},{10,11... | collective-permute-start | bytes 393224 | tf_op jit(solution)/shard_map/ppermute | solution.py:218
  5.2 5.7 %collective-permute-start.1 = (f32[1,64,512]{2,1,0:T(8,128)S(1)}, f32[1,64,512]{2,1,0:T(8,128)S(1)}, u32[]{:S(2)}, u32[]{:S(2)}) collective-permute-start(f32[1,64,512]{2,1,0:T(8,128)S(1)} %get-tuple-element.14), channel_id=1, source_target_pairs={{0,0},{1,2},{2,1},{3,4},{4,3},{5,6},{6,5},{7,8},{8,7},{9,10},{10,9... | collective-permute-start | bytes 393224 | tf_op jit(solution)/shard_map/ppermute | solution.py:218
  5.9 5.0 %collective-permute-start.2 = (f32[16,1,512]{2,1,0:T(1,128)S(1)}, f32[16,1,512]{2,1,0:T(1,128)S(1)}, u32[]{:S(2)}, u32[]{:S(2)}) collective-permute-start(f32[16,1,512]{2,1,0:T(1,128)S(1)} %get-tuple-element.15), channel_id=1, source_target_pairs={{0,32},{32,64},{64,96},{96,128},{128,160},{160,192},{192,224},{224... | collective-permute-start | bytes 98312 | tf_op jit(solution)/shard_map/ppermute | solution.py:207
  5.9 5.0 %collective-permute-start.3 = (f32[16,1,512]{2,1,0:T(1,128)S(1)}, f32[16,1,512]{2,1,0:T(1,128)S(1)}, u32[]{:S(2)}, u32[]{:S(2)}) collective-permute-start(f32[16,1,512]{2,1,0:T(1,128)S(1)} %get-tuple-element.16), channel_id=1, source_target_pairs={{0,480},{32,0},{64,32},{96,64},{128,96},{160,128},{192,160},{224,1... | collective-permute-start | bytes 98312 | tf_op jit(solution)/shard_map/ppermute | solution.py:207

commit v6 on v5

--- a/solution.py
+++ b/solution.py
@@ -188,10 +188,11 @@
     whole_band(bands - 1, None, below)
 
 
-def merge_kernel(parts, out):
+def merge_kernel(order, parts, out):
     count = parts.shape[0]
-    red, green, blue, transmit = (parts[0, j] for j in range(4))
-    for s in range(1, count):
+    nearest, *others = [order.index(slab) for slab in range(count)]
+    red, green, blue, transmit = (parts[nearest, j] for j in range(4))
+    for s in others:
         red = red + transmit * parts[s, 0]
         green = green + transmit * parts[s, 1]
         blue = blue + transmit * parts[s, 2]
@@ -263,16 +264,17 @@
         compiler_params=pltpu.CompilerParams(vmem_limit_bytes=12 * 2**20),
         name="outer",
     )(field, arc_ids, words, inner, layer_1, layer_2, above, below)
-    received = lax.all_to_all(parts, "slab", 0, 0, tiled=True)
+    order = list(range(slabs - 1, -1, -1))
+    received = lax.all_to_all(parts, "slab", 0, 0, axis_index_groups=[order], tiled=True)
     merged = pl.pallas_call(
-        merge_kernel,
+        functools.partial(merge_kernel, order),
         out_shape=shape((slabs, 4, SUB, LANE), f32),
         in_specs=[vmem],
         out_specs=vmem,
         compiler_params=pltpu.CompilerParams(vmem_limit_bytes=4 * 2**20),
         name="merge",
     )(received)
-    pixels = lax.all_to_all(merged, "slab", 0, 0, tiled=True)
+    pixels = lax.all_to_all(merged, "slab", 0, 0, axis_index_groups=[order], tiled=True)
     pixels = pixels.reshape(bands, strips, 4, SUB, LANE).transpose(2, 0, 3, 1, 4)
     return pixels.reshape(4, rows, columns)
 

time: 69.9 us -> 68.5 us (0.980)
  blocking collectives: 56.2 us -> 54.8 us
    all_to_all x2, blocking collectives: 56.2 us -> 54.8 us  [the longest x1 31 us: local(): lax.all_to_all(parts, 'slab', 0, 0, axis_index_groups=[order], tiled=True)]
where the time goes in v6:
time: 68.5 us; the launch traced here: 68.3 us
  blocking collectives  54.8 us (80%)
  starting transfers between devices  5.95 us (9%)
  Pallas kernels  4.97 us (7%)
  local copies, waits for them, and re-layouts  2.46 us (4%)
    all_to_all x1, blocking collectives, local(): lax.all_to_all(parts, 'slab', 0, 0, axis_index_groups=[order], tiled=True)  31 us
    all_to_all x1, blocking collectives, local(): lax.all_to_all(merged, 'slab', 0, 0, axis_index_groups=[order], tiled=True)  23.8 us
    ppermute x2, starting transfers between devices, swapped(): return lax.ppermute(value, axis, list(partner.items()))  4.2 us
    pallas_call x1, Pallas kernels, local(): pl.pallas_call(functools.partial(inner_kernel, step_len), out_shape=[shap...  3.22 us
    ppermute x2, starting transfers between devices, shifted(): lax.ppermute(value, axis, [(i, (i + step) % count) for i in range(count)])  1.75 us
    pallas_call x1, Pallas kernels, local(): pl.pallas_call(functools.partial(outer_kernel, step_len), out_shape=shape...  1.63 us
    unnamed x8, local copies, waits for them, and re-layouts  1.6 us
  transfers between devices with their start and end apart: 4, of which 0 were waited for; matrix products, arithmetic and copies ran while one was open for 0% of the time, Pallas kernels for 5%

profile of v6, /device:TPU:24, one launch (start us, length us, event | category | flops | bytes accessed | tf_op | source)
XLA Modules:
  0.0 68.3 jit_solution(3625405972352343399)
XLA Ops:
  0.0 0.0 copy-start
  0.0 1.6 %copy-done = f32[16,64,512]{2,1,0:T(8,128)S(1)} copy-done((f32[16,64,512]{2,1,0:T(8,128)S(1)}, f32[16,64,512]{2,1,0:T(8,128)}, u32[]{:S(2)}) %copy-start) | copy-done | bytes 2097176
  1.6 0.0 copy-start.1
  1.6 0.0 copy-start.2
  1.6 0.0 copy-start.3
  1.6 3.5 %collective-permute-start = (f32[1,64,512]{2,1,0:T(8,128)S(1)}, f32[1,64,512]{2,1,0:T(8,128)S(1)}, u32[]{:S(2)}, u32[]{:S(2)}) collective-permute-start(f32[1,64,512]{2,1,0:T(8,128)S(1)} %get-tuple-element.13), channel_id=1, source_target_pairs={{0,1},{1,0},{2,3},{3,2},{4,5},{5,4},{6,7},{7,6},{8,9},{9,8},{10,11... | collective-permute-start | bytes 393224 | tf_op jit(solution)/shard_map/ppermute | solution.py:219
  5.2 0.7 collective-permute-start.1
  5.9 0.0 collective-permute-start.2
  5.9 1.7 %collective-permute-start.3 = (f32[16,1,512]{2,1,0:T(1,128)S(1)}, f32[16,1,512]{2,1,0:T(1,128)S(1)}, u32[]{:S(2)}, u32[]{:S(2)}) collective-permute-start(f32[16,1,512]{2,1,0:T(1,128)S(1)} %get-tuple-element.16), channel_id=1, source_target_pairs={{0,480},{32,0},{64,32},{96,64},{128,96},{160,128},{192,160},{224,1... | collective-permute-start | bytes 98312 | tf_op jit(solution)/shard_map/ppermute | solution.py:208
  7.6 0.0 copy-done.1
  7.6 0.0 copy-done.2
  7.6 0.0 copy-done.3
  7.6 3.2 %inner.1 = (s32[3,8,128]{2,1,0:T(8,128)S(1)}, f32[24,4,8,128]{3,2,1,0:T(8,128)S(1)}) custom-call(f32[16,64,512]{2,1,0:T(8,128)S(1)} %copy-done, s32[16,64,512]{2,1,0:T(8,128)S(1)} %copy-done.1, s32[1,64]{1,0:T(1,128)S(1)} %bitcast.7, bf16[6,16]{1,0:T(8,128)(2,1)S(1)} %copy-done.2), custom_call_target="tpu_custom_call" | custom-call | flops 31457280 | bytes 4194304 | tf_op jit(solution)/shard_map/inner/pallas_call | solution.py:243
  10.8 0.0 collective-permute-done.2.above
  10.9 0.0 collective-permute-done.3.below
  10.9 0.0 collective-permute-done.layer_1
  10.9 0.0 collective-permute-done.1.layer_2
  10.9 1.6 %outer.1 = f32[32,4,8,128]{3,2,1,0:T(8,128)S(1)} custom-call(f32[16,64,512]{2,1,0:T(8,128)S(1)} %copy-done, s32[16,64,512]{2,1,0:T(8,128)S(1)} %copy-done.1, s32[3,8,128]{2,1,0:T(8,128)S(1)} %get-tuple-element.11.words, f32[24,4,8,128]{3,2,1,0:T(8,128)S(1)} %get-tuple-element.12.inner, f32[1,64,512]{2,1,0:T(8,128)S(1)} %collective-permute-done.layer_1, ...), custom_call_target="tpu_custom_call" | custom-call | tf_op jit(solution)/shard_map/outer/pallas_call | solution.py:258
  12.5 31.0 %all_to_all.10.parts = f32[32,4,8,128]{3,2,1,0:T(8,128)S(1)} all-to-all(f32[32,4,8,128]{3,2,1,0:T(8,128)S(1)} %outer.1), channel_id=1, replica_groups={{31,30,29,28,27,26,25,24,23,22,21,20,19,18,17,16,15,14,13,12,11,10,9,8,..., dimensions={0} | all-to-all | bytes 1048576 | tf_op jit(solution)/shard_map/all_to_all | solution.py:268
  43.6 0.1 merge.1
  43.7 23.8 %all_to_all.11 = f32[32,4,8,128]{3,2,1,0:T(8,128)S(1)} all-to-all(f32[32,4,8,128]{3,2,1,0:T(8,128)S(1)} %merge.1), channel_id=1, replica_groups={{31,30,29,28,27,26,25,24,23,22,21,20,19,18,17,16,15,14,13,12,11,10,9,8,..., dimensions={0} | all-to-all | bytes 1048576 | tf_op jit(solution)/shard_map/all_to_all | solution.py:277
  67.5 0.9 %copy.7 = f32[4,8,8,4,128]{4,2,3,1,0:T(8,128)} copy(f32[4,8,8,4,128]{4,2,0,3,1:T(8,128)S(1)} %bitcast.8) | data formatting | bytes 1048576 | tf_op jit(solution)/shard_map/transpose | solution.py:278
  (1 shorter events, 0.0 us)
Async XLA Ops:
  0.0 1.6 %copy-start = (f32[16,64,512]{2,1,0:T(8,128)S(1)}, f32[16,64,512]{2,1,0:T(8,128)}, u32[]{:S(2)}) copy-start(f32[16,64,512]{2,1,0:T(8,128)} %vol.3) | copy-start | bytes 6291460
  1.6 6.0 %copy-start.1 = (s32[16,64,512]{2,1,0:T(8,128)S(1)}, s32[16,64,512]{2,1,0:T(8,128)}, u32[]{:S(2)}) copy-start(s32[16,64,512]{2,1,0:T(8,128)} %arc.3) | copy-start | bytes 6291460
  1.6 6.0 %copy-start.2 = (bf16[6,16]{1,0:T(8,128)(2,1)S(1)}, bf16[6,16]{1,0:T(8,128)(2,1)}, u32[]{:S(2)}) copy-start(bf16[6,16]{1,0:T(8,128)(2,1)} %tf.1) | copy-start | bytes 580
  1.6 6.0 %copy-start.3 = (s32[64]{0:T(128)S(1)}, s32[64]{0:T(128)}, u32[]{:S(2)}) copy-start(s32[64]{0:T(128)} %param.6) | copy-start | bytes 772
  1.6 9.2 %collective-permute-start = (f32[1,64,512]{2,1,0:T(8,128)S(1)}, f32[1,64,512]{2,1,0:T(8,128)S(1)}, u32[]{:S(2)}, u32[]{:S(2)}) collective-permute-start(f32[1,64,512]{2,1,0:T(8,128)S(1)} %get-tuple-element.13), channel_id=1, source_target_pairs={{0,1},{1,0},{2,3},{3,2},{4,5},{5,4},{6,7},{7,6},{8,9},{9,8},{10,11... | collective-permute-start | bytes 393224 | tf_op jit(solution)/shard_map/ppermute | solution.py:219
  5.2 5.7 %collective-permute-start.1 = (f32[1,64,512]{2,1,0:T(8,128)S(1)}, f32[1,64,512]{2,1,0:T(8,128)S(1)}, u32[]{:S(2)}, u32[]{:S(2)}) collective-permute-start(f32[1,64,512]{2,1,0:T(8,128)S(1)} %get-tuple-element.14), channel_id=1, source_target_pairs={{0,0},{1,2},{2,1},{3,4},{4,3},{5,6},{6,5},{7,8},{8,7},{9,10},{10,9... | collective-permute-start | bytes 393224 | tf_op jit(solution)/shard_map/ppermute | solution.py:219
  5.9 5.0 %collective-permute-start.2 = (f32[16,1,512]{2,1,0:T(1,128)S(1)}, f32[16,1,512]{2,1,0:T(1,128)S(1)}, u32[]{:S(2)}, u32[]{:S(2)}) collective-permute-start(f32[16,1,512]{2,1,0:T(1,128)S(1)} %get-tuple-element.15), channel_id=1, source_target_pairs={{0,32},{32,64},{64,96},{96,128},{128,160},{160,192},{192,224},{224... | collective-permute-start | bytes 98312 | tf_op jit(solution)/shard_map/ppermute | solution.py:208
  5.9 5.0 %collective-permute-start.3 = (f32[16,1,512]{2,1,0:T(1,128)S(1)}, f32[16,1,512]{2,1,0:T(1,128)S(1)}, u32[]{:S(2)}, u32[]{:S(2)}) collective-permute-start(f32[16,1,512]{2,1,0:T(1,128)S(1)} %get-tuple-element.16), channel_id=1, source_target_pairs={{0,480},{32,0},{64,32},{96,64},{128,96},{160,128},{192,160},{224,1... | collective-permute-start | bytes 98312 | tf_op jit(solution)/shard_map/ppermute | solution.py:208
